TPU v7x, 256 devices: a whole 4x4x8 slice. The times are simulated.
256 devices in a mesh: member: 8 (over y, x_lo), lon: 32 (over x_hi, z, core).
Axes of the slice: x: 4 (x_hi: 2, x_lo: 2; x = x_hi * 2 + x_lo), y: 4, z: 8, core: 2. Of those that a mesh axis runs over, the one named last changes fastest.
Arguments:
- fields: bfloat16 [8, 641, 20, 1440], P('member', None, None, 'lon'), may hold values from -6 to 6
- weight: bfloat16 [5, 5, 73, 641], replicated, may hold values from -0.046875 to 0.046875
- out_bias: float32 [73], replicated, may hold values from -3 to 3
- observed: float32 [73, 16, 1440], P(None, None, 'lon'), may hold values from -6 to 6
- widths: float32 [73], replicated, may hold values from 0.5 to 2
- owner_start: int32 [32, 9], P('lon'), may hold values from 0 to 16, as said below
Outputs:
- out_grad: bfloat16 [8, 73, 16, 1440], P('member', None, None, 'lon')
- owned_score: float32 [32, 8, 270], P('lon', 'member')
- weight_grad: float32 [5, 5, 73, 641], replicated
- bias_grad: float32 [73], replicated
Inputs may be any that keep to these rules, and one draw needn't show every extreme that they name: Each row owner_start[l] starts at 0, never falls and ends at 16; owner r of longitude group l holds blocks owner_start[l, r] to owner_start[l, r + 1] - 1, at most 6 of them, and in every group some owner holds exactly 6.
All inputs are finite; a program needn't handle non-finite values.
Results may differ from a plain program's by a relative error of at most 0.0063.
Values may be sent and summed in bfloat16 or wider, within the bound.
A program may use at most 128 MiB of HBM per device.

v0:
```python
import math

import jax
import jax.numpy as jnp
from jax import lax
from jax.sharding import PartitionSpec as P

BLOCK = 45


def extended(block, sides, width):
    for axis, dim in sides:
        count = lax.axis_size(axis)
        forward = [(i, i + 1) for i in range(count - 1)]
        forward.append((count - 1, 0))
        backward = [(target, source) for source, target in forward]
        low = lax.ppermute(
            lax.slice_in_dim(block, block.shape[dim] - width, None, axis=dim), axis, forward
        )
        high = lax.ppermute(lax.slice_in_dim(block, 0, width, axis=dim), axis, backward)
        block = jnp.concatenate([low, block, high], axis=dim)
    return block


def kernel_terms(values, target, widths):
    members = values.astype(jnp.float32)
    ensemble = members.shape[0]
    inverse = (1.0 / (widths * widths))[:, None]
    spread = members[:, None] - members[None, :]
    kernel_pair = jnp.exp(-0.5 * spread * spread * inverse)
    misfit = members - target[None]
    kernel_obs = jnp.exp(-0.5 * misfit * misfit * inverse)
    per_channel = (
        jnp.sum(kernel_pair, axis=(0, 1)) / (2.0 * ensemble * ensemble)
        - jnp.sum(kernel_obs, axis=0) / ensemble
    )
    scores = jnp.mean(per_channel, axis=0)
    gradient = inverse * (misfit * kernel_obs - jnp.sum(kernel_pair * spread, axis=1) / ensemble)
    return (scores, gradient.astype(jnp.bfloat16))


def tap_stack(gradients, rows_in, padded_width):
    leading = gradients.ndim - 2
    padded = jnp.pad(gradients, [(0, 0)] * leading + [(4, 4), (4, 4)])
    pieces = [
        padded[..., 4 - row_tap : 4 - row_tap + rows_in, 4 - col_tap : 4 - col_tap + padded_width]
        for row_tap in range(5)
        for col_tap in range(5)
    ]
    return jnp.stack(pieces, axis=-4)


def body(fields, weight, out_bias, observed, widths, owner_start):
    local_members, in_chan, rows_in, lon_dev = fields.shape
    out_chan = weight.shape[2]
    rows_out = rows_in - 4
    padded_width = lon_dev + 4
    padded = extended(fields, (("lon", 3),), 2)
    flat_field = padded.reshape(local_members, in_chan, rows_in * padded_width)
    flat_weight = weight.reshape(25 * out_chan, in_chan)
    tap_sums = jnp.einsum(
        "kc,mcp->mkp", flat_weight, flat_field, preferred_element_type=jnp.float32
    )
    tap_sums = tap_sums.reshape(local_members, 5, 5, out_chan, rows_in, padded_width)
    convolved = jnp.broadcast_to(
        out_bias[None, :, None, None], (local_members, out_chan, rows_out, lon_dev)
    )
    for row_tap in range(5):
        for col_tap in range(5):
            convolved = (
                convolved
                + tap_sums[
                    :,
                    row_tap,
                    col_tap,
                    :,
                    row_tap : row_tap + rows_out,
                    col_tap : col_tap + lon_dev,
                ]
            )
    outputs = convolved.astype(jnp.bfloat16)
    owners = lax.axis_size("member")
    own_rank = lax.axis_index("member")
    blocks = rows_out * lon_dev // BLOCK
    capacity = max(2, 3 * blocks // owners)
    starts = owner_start[0]
    slot_index = jnp.arange(capacity, dtype=jnp.int32)
    owned_blocks = starts[1:] - starts[:-1]
    filled = slot_index[None, :] < owned_blocks[:, None]
    global_block = starts[:-1, None] + slot_index[None, :]
    even_blocks = blocks // owners
    sending = outputs.reshape(local_members, out_chan, owners, even_blocks * BLOCK)
    arrived = lax.all_to_all(sending, "member", split_axis=2, concat_axis=0, tiled=True).reshape(
        -1, out_chan, even_blocks * BLOCK
    )
    target = lax.dynamic_slice_in_dim(observed, own_rank * even_blocks, even_blocks, 1)
    target = target.reshape(out_chan, even_blocks * BLOCK)
    scores, gradients = kernel_terms(arrived, target, widths)
    local_grad = lax.all_to_all(
        gradients.reshape(-1, out_chan, 1, even_blocks * BLOCK),
        "member",
        split_axis=0,
        concat_axis=2,
        tiled=True,
    )
    from_self = filled & (global_block // even_blocks == own_rank)
    local_index = jnp.clip(global_block - own_rank * even_blocks, 0, even_blocks - 1)
    parcel = jnp.take(scores.reshape(even_blocks, BLOCK), local_index.reshape(-1), axis=0)
    parcel = jnp.where(from_self[..., None], parcel.reshape(owners, capacity, BLOCK), 0.0)
    gathered = lax.all_to_all(
        parcel.reshape(owners, capacity * BLOCK), "member", split_axis=0, concat_axis=0, tiled=True
    )
    owned_score = jnp.sum(gathered, axis=0).reshape(1, 1, capacity * BLOCK)
    out_grad = local_grad.reshape(local_members, out_chan, rows_out, lon_dev)
    stacked = tap_stack(out_grad, rows_in, padded_width).reshape(
        local_members, 25 * out_chan, rows_in * padded_width
    )
    weight_part = lax.dot_general(
        stacked, flat_field, (((0, 2), (0, 2)), ((), ())), preferred_element_type=jnp.float32
    )
    bias_part = jnp.sum(out_grad.astype(jnp.float32), axis=(0, 2, 3))
    factor = 1.0 / math.sqrt(local_members * owners * rows_out * lon_dev * lax.axis_size("lon"))
    weight_sum, bias_sum = lax.psum((weight_part, bias_part), ("member", "lon"))
    weight_grad = (weight_sum * factor).reshape(5, 5, out_chan, in_chan)
    bias_grad = bias_sum * factor
    return (out_grad, owned_score, weight_grad, bias_grad)


def solution(mesh):
    in_specs = (P("member", None, None, "lon"), P(), P(), P(None, None, "lon"), P(), P("lon", None))
    out_specs = (P("member", None, None, "lon"), P("lon", "member", None), P(), P())
    return jax.shard_map(body, mesh=mesh, in_specs=in_specs, out_specs=out_specs, check_vma=False)
```

profile of v0, /device:TPU:1, one launch (start us, length us, event | category | flops | bytes accessed | tf_op | source)
XLA Modules:
  0.0 438.3 jit_solution(3207606397779355564)
XLA Ops:
  7.2 1.2 fusion.72
  8.4 3.1 collective-permute-start
  11.5 0.3 collective-permute-start.1
  11.8 0.7 multiply_divide_fusion
  12.5 4.9 %reshape.609 = bf16[1825,641]{1,0:T(8,128)(2,1)} reshape(bf16[5,5,73,641]{3,2,1,0:T(8,128)(2,1)} %param.7) | data formatting | bytes 4679300 | tf_op jit(solution)/shard_map/reshape | solution.py:60
  17.4 2.4 pad_maximum_fusion
  19.8 1.9 reshape.608
  21.6 8.4 %convolution_bitcast_fusion = f32[1,1825,980]{2,1,0:T(8,128)} fusion(bf16[641,980]{0,1:T(8,128)(2,1)} %reshape.608, bf16[1825,641]{1,0:T(8,128)(2,1)} %reshape.609), kind=kOutput, calls=%fused_computation.4 | convolution fusion | flops 2292857088 | bytes 10750010 | tf_op jit(solution)/shard_map/kc,mcp->mkp/dot_general | solution.py:61
  30.0 8.7 %copy.64 = f32[1,1825,980]{1,2,0:T(8,128)} copy(f32[1,1825,980]{2,1,0:T(8,128)} %convolution_bitcast_fusion) | data formatting | bytes 14308000 | tf_op jit(solution)/shard_map/kc,mcp->mkp/transpose | solution.py:61
  38.7 14.5 %reshape.610 = f32[1,5,5,73,20,49]{3,2,1,5,4,0:T(8,128)} reshape(f32[1,1825,980]{1,2,0:T(8,128)} %copy.64) | data formatting | bytes 14308000 | tf_op jit(solution)/shard_map/reshape | solution.py:64
  53.2 22.3 %fusion.70 = (f32[1,1,1,73,16,45]{3,2,1,5,4,0:T(1,128)S(1)}, f32[1,1,1,73,16,45]{3,2,1,5,4,0:T(1,128)S(1)}, f32[1,1,1,73,16,45]{3,2,1,5,4,0:T(1,128)S(1)}, f32[1...) fusion(f32[1,5,5,73,20,49]{3,2,1,5,4,0:T(8,128)} %reshape.610), kind=kLoop, calls=%fused_computation.130 | loop fusion | bytes 7989120 | tf_op jit(solution)/shard_map/slice | solution.py:72
  75.5 9.1 %fusion.71 = (f32[1,1,1,73,16,45]{3,2,1,5,4,0:T(1,128)S(1)}, f32[1,1,1,73,16,45]{3,2,1,5,4,0:T(1,128)S(1)}, f32[1,1,1,73,16,45]{3,2,1,5,4,0:T(1,128)S(1)}, f32[1...) fusion(f32[1,5,5,73,20,49]{3,2,1,5,4,0:T(8,128)} %reshape.610), kind=kLoop, calls=%fused_computation.131 | loop fusion | bytes 2522880 | tf_op jit(solution)/shard_map/slice | solution.py:72
  84.6 3.6 add_convert_fusion
  88.2 1.0 copy.65
  89.2 4.8 %all-to-all-start = ((bf16[1,73,8,90]{3,1,0,2:T(8,128)(2,1)}), bf16[1,73,8,90]{3,1,0,2:T(8,128)(2,1)S(1)}, u32[]{:S(2)}, u32[]{:S(2)}) async-start(bf16[1,73,8,90]{3,1,0,2:T(8,128)(2,1)} %copy.65), calls=%async_computation | async-start | bytes 327680 | tf_op jit(solution)/shard_map/all_to_all | solution.py:93
  94.1 0.1 copy.80
  94.3 0.1 reshape.627
  94.4 5.4 %all-to-all-done = bf16[1,73,8,90]{3,1,0,2:T(8,128)(2,1)S(1)} async-done(((bf16[1,73,8,90]{3,1,0,2:T(8,128)(2,1)}), bf16[1,73,8,90]{3,1,0,2:T(8,128)(2,1)S(1)}, u32[]{:S(2)}, u32[]{:S(2)}) %all-to-all-start) | async-done | bytes 105152 | tf_op jit(solution)/shard_map/all_to_all | solution.py:93
  99.8 1.5 fusion.2
  101.3 0.2 fusion.8
  101.5 8.1 %all_to_all.30 = bf16[8,73,1,90]{3,1,2,0:T(8,128)(2,1)S(1)} all-to-all(bf16[8,73,1,90]{3,1,2,0:T(8,128)(2,1)S(1)} %copy.72), channel_id=1, replica_groups=mesh['member'=8,'lon'=32] {'member'}, dimensions={0} | all-to-all | bytes 210240 | tf_op jit(solution)/shard_map/all_to_all | solution.py:99
  109.6 0.6 convert_reduce_fusion
  110.2 0.2 copy.74
  110.6 0.1 fusion.17
  110.7 0.1 fusion.19
  110.8 0.1 fusion.21
  110.9 0.1 fusion.23
  111.0 0.1 fusion.25
  111.1 0.1 fusion.27
  111.2 0.1 fusion.29
  111.3 0.1 fusion.31
  111.4 0.1 fusion.33
  111.5 0.1 fusion.35
  111.6 0.1 fusion.37
  111.7 0.1 fusion.39
  111.8 0.1 fusion.41
  111.9 0.1 fusion.43
  112.1 0.1 fusion.47
  112.2 0.1 fusion.49
  112.3 0.1 fusion.51
  112.4 0.1 fusion.53
  112.6 0.1 fusion.57
  112.7 0.1 fusion.59
  112.8 0.1 fusion.61
  112.9 0.1 fusion.63
  113.0 5.8 %copy.77 = bf16[1,25,73,20,49]{2,1,4,3,0:T(8,128)(2,1)} copy(bf16[1,25,73,20,49]{2,4,3,1,0:T(8,128)(2,1)S(1)} %fusion.63) | data formatting | bytes 7154000 | tf_op jit(solution)/shard_map/stack | solution.py:50
  118.9 13.7 %reshape.613 = bf16[1825,980]{0,1:T(8,128)(2,1)} reshape(bf16[1,25,73,20,49]{2,1,4,3,0:T(8,128)(2,1)} %copy.77) | data formatting | bytes 7154000 | tf_op jit(solution)/shard_map/reshape.9
  132.6 7.3 %fusion.73 = f32[1825,641]{0,1:T(8,128)} fusion(bf16[1825,980]{0,1:T(8,128)(2,1)} %reshape.613, bf16[641,980]{0,1:T(8,128)(2,1)S(1)} %copy-done.2), kind=kOutput, calls=%fused_computation.133 | convolution fusion | flops 2292857088 | bytes 9512660 | tf_op jit(solution)/shard_map/dot_general | solution.py:118
  140.1 0.1 min.9
  140.2 0.1 compare_and_fusion
  140.4 0.1 broadcast_in_dim.41
  140.6 0.1 broadcast_in_dim.43
  140.7 0.2 fusion.13
  140.9 0.1 div.58
  141.0 0.6 gather_fusion
  141.7 7.4 %all_to_all.31 = f32[8,1,270]{2,1,0:T(1,128)S(1)} all-to-all(f32[8,1,270]{2,1,0:T(1,128)S(1)} %copy.76), channel_id=1, replica_groups=mesh['member'=8,'lon'=32] {'member'}, dimensions={0} | all-to-all | bytes 17280 | tf_op jit(solution)/shard_map/all_to_all | solution.py:110
  149.1 0.6 reshape.612
  149.7 0.7 copy.79
  150.4 81.8 %psum.15 = f32[73]{0:T(128)S(1)} all-reduce(f32[73]{0:T(128)S(1)} %get-tuple-element.30), channel_id=1, replica_groups=mesh['member'=8,'lon'=32] {'member','lon'}, use_global_device_ids=true, to_apply=%region_7.8 | all-reduce | flops 73 | bytes 584 | tf_op jit(solution)/shard_map/psum | solution.py:123
  232.2 0.5 broadcast_multiply_fusion.1
  232.7 181.3 %all-reduce.3.cloned.1.call-done = f32[1825,641]{0,1:T(8,128)} async-done(((f32[1825,641]{0,1:T(8,128)}), f32[1825,641]{0,1:T(8,128)}) %all-reduce.3.cloned.1.call-update) | async-done | bytes 4679316 | tf_op jit(solution)/shard_map/psum | solution.py:123
  414.0 5.1 %broadcast_multiply_fusion = f32[1825,641]{0,1:T(8,128)} fusion(f32[1825,641]{0,1:T(8,128)} %all-reduce.3.cloned.1.call-done), kind=kLoop, calls=%fused_computation.5 | loop fusion | flops 1169825 | bytes 9358600 | tf_op jit(solution)/shard_map/mul | solution.py:124
  419.1 6.1 %copy.78 = f32[1825,641]{1,0:T(8,128)} copy(f32[1825,641]{0,1:T(8,128)} %broadcast_multiply_fusion) | data formatting | bytes 9358600 | tf_op jit(solution)/shard_map/mul | solution.py:124
  425.2 6.2 %reshape.614 = f32[5,5,73,641]{3,2,1,0:T(8,128)} reshape(f32[1825,641]{1,0:T(8,128)} %copy.78) | data formatting | bytes 9358600 | tf_op jit(solution)/shard_map/reshape | solution.py:124
  (35 shorter events, 1.0 us)
Async XLA Ops:
  7.2 86.9 %copy-start = (f32[73,16,45]{0,1,2:T(8,128)S(1)}, f32[73,16,45]{0,1,2:T(8,128)}, u32[]{:S(2)}) copy-start(f32[73,16,45]{0,1,2:T(8,128)} %param.9) | copy-start | bytes 630724
  8.4 9.0 %collective-permute-start = (bf16[1,641,20,2]{1,3,2,0:T(2,128)(2,1)S(1)}, bf16[1,641,20,2]{1,3,2,0:T(2,128)(2,1)S(1)}, u32[]{:S(2)}, u32[]{:S(2)}) collective-permute-start(bf16[1,641,20,2]{1,3,2,0:T(2,128)(2,1)S(1)} %get-tuple-element.57), channel_id=1, source_target_pairs={{0,1},{1,2},{2,3},{3,4},{4,5},{5,6},{6,7},{7,8},{8,9},{9,10},{10,1... | collective-permute-start | bytes 153848 | tf_op jit(solution)/shard_map/ppermute | solution.py:17
  11.5 5.9 %collective-permute-start.1 = (bf16[1,641,20,2]{1,3,2,0:T(2,128)(2,1)S(1)}, bf16[1,641,20,2]{1,3,2,0:T(2,128)(2,1)S(1)}, u32[]{:S(2)}, u32[]{:S(2)}) collective-permute-start(bf16[1,641,20,2]{1,3,2,0:T(2,128)(2,1)S(1)} %get-tuple-element.58), channel_id=1, source_target_pairs={{1,0},{2,1},{3,2},{4,3},{5,4},{6,5},{7,6},{8,7},{9,8},{10,9},{11,1... | collective-permute-start | bytes 153848 | tf_op jit(solution)/shard_map/ppermute | solution.py:20
  53.2 31.4 %copy-start.3 = (f32[73]{0:T(128)S(1)}, f32[73]{0:T(128)}, u32[]{:S(2)}) copy-start(f32[73]{0:T(128)} %param.8) | copy-start | bytes 880
  89.2 10.5 %all-to-all-start = ((bf16[1,73,8,90]{3,1,0,2:T(8,128)(2,1)}), bf16[1,73,8,90]{3,1,0,2:T(8,128)(2,1)S(1)}, u32[]{:S(2)}, u32[]{:S(2)}) async-start(bf16[1,73,8,90]{3,1,0,2:T(8,128)(2,1)} %copy.65), calls=%async_computation | async-start | bytes 327680 | tf_op jit(solution)/shard_map/all_to_all | solution.py:93
  94.0 319.9 %all-reduce.3.cloned.1.call-start = ((), (), s32[]{:S(2)}) async-start(), calls=%async_computation.3 | async-start | bytes 9953280 | tf_op jit(solution)/shard_map/psum | solution.py:123
  118.9 13.7 %copy-start.2 = (bf16[641,980]{0,1:T(8,128)(2,1)S(1)}, bf16[641,980]{0,1:T(8,128)(2,1)}, u32[]{:S(2)}) copy-start(bf16[641,980]{0,1:T(8,128)(2,1)} %reshape.608) | copy-start | bytes 3769084
  132.6 7.4 %copy-start.4 = (s32[1,9]{1,0:T(1,128)S(1)}, s32[1,9]{1,0:T(1,128)}, u32[]{:S(2)}) copy-start(s32[1,9]{1,0:T(1,128)} %param.11) | copy-start | bytes 112
  419.1 12.3 %copy-start.1 = (f32[73,16,45]{0,1,2:T(8,128)S(1)}, f32[73,16,45]{0,1,2:T(8,128)}, u32[]{:S(2)}) copy-start(f32[73,16,45]{0,1,2:T(8,128)} %param.9) | copy-start | bytes 630724
Sparse Core Ops, SparseCore 0:
  140.1 273.8 all-reduce.2
where the time goes:
time: 440 us; the launch traced here: 438 us
  waiting for transfers between devices  187 us (42%)
  local copies, waits for them, and re-layouts  101 us (23%)
  blocking collectives  97.2 us (22%)
  matrix products  15.7 us (4%)
  other arithmetic  15.1 us (3%)
  between operations  14.2 us (3%)
  starting transfers between devices  8.26 us (2%)
    psum x1, waiting for transfers between devices, body(): weight_sum, bias_sum = lax.psum((weight_part, bias_part), ('member', 'lon'))  181 us
    psum x1, blocking collectives, body(): weight_sum, bias_sum = lax.psum((weight_part, bias_part), ('member', 'lon'))  81.8 us
    slice x2, local copies, waits for them, and re-layouts, body(): tap_sums[:, row_tap, col_tap, :, row_tap:row_tap + rows_out, col_tap:col_...  31.4 us
    another operation x2, local copies, waits for them, and re-layouts  15.6 us
    reshape x1, local copies, waits for them, and re-layouts, body(): tap_sums.reshape(local_members, 5, 5, out_chan, rows_in, padded_width)  14.5 us
  transfers between devices with their start and end apart: 4, of which 2 were waited for; matrix products, arithmetic and copies ran while one was open for 2% of the time, Pallas kernels for 0%

commit v1 on v0

--- a/solution.py
+++ b/solution.py
@@ -3,7 +3,198 @@
 import jax
 import jax.numpy as jnp
 from jax import lax
+from jax.experimental import pallas as pl
 from jax.sharding import PartitionSpec as P
+from jax.experimental.pallas import tpu as pltpu
+
+MESH = pl.DeviceIdType.MESH
+ROWS = 2048
+LANES = 128
+PARTS = 3
+COLS = 2 * PARTS * LANES
+ORDERS = (("x", "y", "z"), ("y", "x", "z"), ("z", "x", "y"))
+
+
+def position():
+    member = lax.axis_index("member")
+    lon = lax.axis_index("lon")
+    return {
+        "x": (lon // 16) * 2 + member % 2,
+        "y": member // 2,
+        "z": (lon // 2) % 8,
+        "core": lon % 2,
+    }
+
+
+EXTENT = {"x": 4, "y": 4, "z": 8, "core": 2}
+
+
+def device(at):
+    return (at["y"] * 2 + at["x"] % 2, (at["x"] // 2) * 16 + at["z"] * 2 + at["core"])
+
+
+def moved(at, axis, delta):
+    there = dict(at)
+    there[axis] = lax.rem(at[axis] + delta, EXTENT[axis])
+    return there
+
+
+def send(src, dst, send_sem, recv_sem, at):
+    copy = pltpu.make_async_remote_copy(
+        src_ref=src, dst_ref=dst, send_sem=send_sem, recv_sem=recv_sem,
+        device_id=device(at), device_id_type=MESH,
+    )
+    copy.start()
+
+
+def finish(ref, send_sem, recv_sem, at):
+    copy = pltpu.make_async_remote_copy(
+        src_ref=ref, dst_ref=ref, send_sem=send_sem, recv_sem=recv_sem,
+        device_id=device(at), device_id_type=MESH,
+    )
+    return copy
+
+
+def greet(at, axes):
+    barrier = pltpu.get_barrier_semaphore()
+    count = 0
+    for axis in axes:
+        for delta in range(1, EXTENT[axis]):
+            pl.semaphore_signal(
+                barrier, inc=1, device_id=device(moved(at, axis, delta)), device_id_type=MESH
+            )
+            count += 1
+    pl.semaphore_wait(barrier, count)
+
+
+def stage_rows(order):
+    rows, sizes = ROWS, []
+    for axis in order:
+        rows //= EXTENT[axis]
+        sizes.append(rows)
+    return sizes
+
+
+def all_reduce(at, dw, out, core_rx, cur, rxs, send_sems, recv_sems):
+    core = at["core"]
+    partner = moved(at, "core", 1)
+    for k in range(PARTS):
+        send(dw.at[1 - core, k], core_rx.at[k], send_sems.at[k, 0], recv_sems.at[k, 0], partner)
+    row = [0] * PARTS
+    sizes = [stage_rows(order) for order in ORDERS]
+
+    def launch(k, s):
+        axis, rows = ORDERS[k][s], sizes[k][s]
+        for delta in range(1, EXTENT[axis]):
+            there = moved(at, axis, delta)
+            source = cur[k][s].at[pl.ds(pl.multiple_of(there[axis] * rows, 16), rows)]
+            send(source, rxs[k][s].at[delta - 1], send_sems.at[k, s + 1], recv_sems.at[k, s + 1], there)
+
+    for k in range(PARTS):
+        finish(core_rx.at[k], send_sems.at[k, 0], recv_sems.at[k, 0], partner).wait_recv()
+        step = 256
+
+        def add(i, _, k=k):
+            here = pl.ds(pl.multiple_of(i * step, step), step)
+            total = dw[core, k, here, :].astype(jnp.float32) + core_rx[k, here, :].astype(jnp.float32)
+            cur[k][0][here, :] = total.astype(jnp.bfloat16)
+            return 0
+
+        lax.fori_loop(0, ROWS // step, add, 0)
+        launch(k, 0)
+    for s in range(3):
+        for k in range(PARTS):
+            axis, rows = ORDERS[k][s], sizes[k][s]
+            finish(rxs[k][s], send_sems.at[k, s + 1], recv_sems.at[k, s + 1], partner).wait_recv()
+            row[k] = row[k] + at[axis] * rows
+            base = pl.multiple_of(at[axis] * rows, 16)
+            step = min(rows, 128)
+            lane = pl.ds(pl.multiple_of(core * (PARTS * LANES) + k * LANES, LANES), LANES)
+
+            def add(i, _, k=k, s=s, axis=axis, base=base, step=step, lane=lane):
+                total = cur[k][s][pl.ds(pl.multiple_of(base + i * step, 16), step), :].astype(jnp.float32)
+                here = pl.ds(pl.multiple_of(i * step, 16), step)
+                for slot in range(EXTENT[axis] - 1):
+                    total = total + rxs[k][s][slot, here, :].astype(jnp.float32)
+                if s < 2:
+                    cur[k][s + 1][here, :] = total.astype(jnp.bfloat16)
+                else:
+                    out[pl.ds(pl.multiple_of(row[k], 16), step), lane] = total.astype(jnp.bfloat16)
+                return 0
+
+            if rows == step:
+                add(0, 0)
+            else:
+                lax.fori_loop(0, rows // step, add, 0)
+            if s < 2:
+                launch(k, s + 1)
+            else:
+                gather(at, out, k, 2, row, sizes, send_sems, recv_sems)
+    for s in (2, 1, 0):
+        for k in range(PARTS):
+            axis, rows = ORDERS[k][s], sizes[k][s]
+            whole = rxs[k][s]
+            finish(whole, send_sems.at[k, 4 + s], recv_sems.at[k, 4 + s], partner).wait_recv()
+            row[k] = row[k] - at[axis] * rows
+            if s > 0:
+                gather(at, out, k, s - 1, row, sizes, send_sems, recv_sems)
+            else:
+                lane = pl.ds(pl.multiple_of(core * (PARTS * LANES) + k * LANES, LANES), LANES)
+                send(out.at[:, lane], out.at[:, lane], send_sems.at[k, 7], recv_sems.at[k, 7], partner)
+    for k in range(PARTS):
+        finish(core_rx.at[k], send_sems.at[k, 7], recv_sems.at[k, 7], partner).wait_recv()
+    for k in range(PARTS):
+        finish(core_rx.at[k], send_sems.at[k, 0], recv_sems.at[k, 0], partner).wait_send()
+        finish(core_rx.at[k], send_sems.at[k, 7], recv_sems.at[k, 7], partner).wait_send()
+        for s in range(3):
+            finish(rxs[k][s], send_sems.at[k, s + 1], recv_sems.at[k, s + 1], partner).wait_send()
+            finish(rxs[k][s], send_sems.at[k, s + 4], recv_sems.at[k, s + 4], partner).wait_send()
+
+
+def gather(at, out, k, s, row, sizes, send_sems, recv_sems):
+    axis, rows = ORDERS[k][s], sizes[k][s]
+    lane = pl.ds(pl.multiple_of(at["core"] * (PARTS * LANES) + k * LANES, LANES), LANES)
+    block = out.at[pl.ds(pl.multiple_of(row[k], 16), rows), lane]
+    for delta in range(1, EXTENT[axis]):
+        send(block, block, send_sems.at[k, 4 + s], recv_sems.at[k, 4 + s], moved(at, axis, delta))
+
+
+def reduce_scratch():
+    shapes = [pltpu.VMEM((PARTS, ROWS, LANES), jnp.bfloat16)]
+    for order in ORDERS:
+        rows = ROWS
+        for size in stage_rows(order):
+            shapes.append(pltpu.VMEM((rows, LANES), jnp.bfloat16))
+            rows = size
+    for order in ORDERS:
+        for axis, size in zip(order, stage_rows(order)):
+            shapes.append(pltpu.VMEM((EXTENT[axis] - 1, size, LANES), jnp.bfloat16))
+    shapes += [pltpu.SemaphoreType.DMA((PARTS, 8)), pltpu.SemaphoreType.DMA((PARTS, 8))]
+    return shapes
+
+
+def reduce_kernel(dw, out, *scratch):
+    core_rx, rest = scratch[0], scratch[1:]
+    cur = [rest[3 * k : 3 * k + 3] for k in range(PARTS)]
+    rxs = [rest[9 + 3 * k : 12 + 3 * k] for k in range(PARTS)]
+    send_sems, recv_sems = rest[18], rest[19]
+    at = position()
+    greet(at, ("core", "x", "y", "z"))
+    all_reduce(at, dw, out, core_rx, cur, rxs, send_sems, recv_sems)
+
+
+def reduced(dw):
+    return pl.pallas_call(
+        reduce_kernel,
+        out_shape=jax.ShapeDtypeStruct((ROWS, COLS), jnp.bfloat16),
+        in_specs=[pl.BlockSpec(memory_space=pltpu.VMEM)],
+        out_specs=pl.BlockSpec(memory_space=pltpu.VMEM),
+        scratch_shapes=reduce_scratch(),
+        compiler_params=pltpu.CompilerParams(
+            collective_id=1, has_side_effects=True, vmem_limit_bytes=48 * 1024 * 1024
+        ),
+        cost_estimate=pl.CostEstimate(flops=2048 * 768 * 4, bytes_accessed=8 << 20, transcendentals=0),
+    )(dw)
 
 BLOCK = 45
 
@@ -119,8 +310,17 @@
         stacked, flat_field, (((0, 2), (0, 2)), ((), ())), preferred_element_type=jnp.float32
     )
     bias_part = jnp.sum(out_grad.astype(jnp.float32), axis=(0, 2, 3))
+    terms = jnp.pad(
+        weight_part.reshape(25, out_chan, in_chan), ((0, 0), (0, 80 - out_chan), (0, COLS - in_chan))
+    )
+    bias_column = jnp.pad(bias_part, (0, 80 - out_chan))
+    terms = terms.at[:, :, in_chan].set(bias_column[None])
+    terms = jnp.pad(terms.reshape(2000, COLS), ((0, ROWS - 2000), (0, 0))).astype(jnp.bfloat16)
+    terms = jnp.transpose(terms.reshape(ROWS, 2, PARTS, LANES), (1, 2, 0, 3))
+    summed = reduced(terms)[:2000].reshape(25, 80, COLS)
     factor = 1.0 / math.sqrt(local_members * owners * rows_out * lon_dev * lax.axis_size("lon"))
-    weight_sum, bias_sum = lax.psum((weight_part, bias_part), ("member", "lon"))
+    weight_sum = summed[:, :out_chan, :in_chan].astype(jnp.float32)
+    bias_sum = summed[12, :out_chan, in_chan].astype(jnp.float32)
     weight_grad = (weight_sum * factor).reshape(5, 5, out_chan, in_chan)
     bias_grad = bias_sum * factor
     return (out_grad, owned_score, weight_grad, bias_grad)

time: 440 us -> 212 us (0.48)
  waiting for transfers between devices: 187 us -> 14.8 us
  blocking collectives: 97.2 us -> 0 us
  Pallas kernels: 0 us -> 60.5 us
  between operations: 14.2 us -> 0.88 us
  local copies, waits for them, and re-layouts: 101 us -> 92.3 us
  starting transfers between devices: 8.26 us -> 14.9 us
    psum x1 -> x0, waiting for transfers between devices: 181 us -> none  [body(): weight_sum, bias_sum = lax.psum((weight_part, bias_part), ('member', 'lon'))]
    psum x1 -> x0, blocking collectives: 81.8 us -> none  [body(): weight_sum, bias_sum = lax.psum((weight_part, bias_part), ('member', 'lon'))]
    pallas_call x0 -> x1, Pallas kernels: none -> 60.5 us  [reduced(): pl.pallas_call(reduce_kernel, out_shape=jax.ShapeDtypeStruct((ROWS, COLS)...]
    all_to_all x2 -> x0, blocking collectives: 15.5 us -> none  [the longest x1 8.07 us: body(): lax.all_to_all(gradients.reshape(-1, out_chan, 1, even_blocks * BLOCK), '...]
    another operation x2, local copies, waits for them, and re-layouts: 15.6 us -> 2.12 us
    all_to_all x0 -> x2, waiting for transfers between devices: none -> 9.08 us  [the longest x1 5.01 us: body(): lax.all_to_all(gradients.reshape(-1, out_chan, 1, even_blocks * BLOCK), '...]
    all_to_all x0 -> x2, starting transfers between devices: none -> 6.72 us  [the longest x1 3.38 us: body(): lax.all_to_all(gradients.reshape(-1, out_chan, 1, even_blocks * BLOCK), '...]
    mul x1 -> x0, local copies, waits for them, and re-layouts: 6.12 us -> none  [body(): weight_grad = (weight_sum * factor).reshape(5, 5, out_chan, in_chan)]
  transfers between devices with their start and end apart: 4 -> 5, of which waited for: 2 -> 3; matrix products, arithmetic and copies ran while one was open for 2% -> 4% of each run, Pallas kernels for 0% -> 0%
where the time goes in v1:
time: 212 us; the launch traced here: 210 us
  local copies, waits for them, and re-layouts  92.3 us (44%)
  Pallas kernels  60.5 us (29%)
  starting transfers between devices  14.9 us (7%)
  waiting for transfers between devices  14.8 us (7%)
  other arithmetic  13.8 us (7%)
  matrix products  13.3 us (6%)
    pallas_call x1, Pallas kernels, reduced(): pl.pallas_call(reduce_kernel, out_shape=jax.ShapeDtypeStruct((ROWS, COLS)...  60.5 us
    slice x2, local copies, waits for them, and re-layouts, body(): tap_sums[:, row_tap, col_tap, :, row_tap:row_tap + rows_out, col_tap:col_...  31.5 us
    reshape x1, local copies, waits for them, and re-layouts, body(): tap_sums.reshape(local_members, 5, 5, out_chan, rows_in, padded_width)  14.5 us
    transpose x1, local copies, waits for them, and re-layouts, body(): jnp.einsum('kc,mcp->mkp', flat_weight, flat_field, preferred_element_type...  8.75 us
    dot_general x1, matrix products, body(): jnp.einsum('kc,mcp->mkp', flat_weight, flat_field, preferred_element_type...  8.36 us
    all_to_all x1, waiting for transfers between devices, body(): lax.all_to_all(sending, 'member', split_axis=2, concat_axis=0, tiled=True)  5.67 us
    all_to_all x1, waiting for transfers between devices, body(): lax.all_to_all(gradients.reshape(-1, out_chan, 1, even_blocks * BLOCK), '...  5.01 us
    dot_general x1, matrix products, body(): lax.dot_general(stacked, flat_field, (((0, 2), (0, 2)), ((), ())), prefer...  4.93 us
  transfers between devices with their start and end apart: 5, of which 3 were waited for; matrix products, arithmetic and copies ran while one was open for 4% of the time, Pallas kernels for 0%

profile of v1, /device:TPU:1, one launch (start us, length us, event | category | flops | bytes accessed | tf_op | source)
XLA Modules:
  0.0 210.4 jit_solution(9622153159278593966)
XLA Ops:
  0.6 1.2 fusion.78
  1.9 3.1 %collective-permute-start = (bf16[1,641,20,2]{1,3,2,0:T(2,128)(2,1)S(1)}, bf16[1,641,20,2]{1,3,2,0:T(2,128)(2,1)S(1)}, u32[]{:S(2)}, u32[]{:S(2)}) collective-permute-start(bf16[1,641,20,2]{1,3,2,0:T(2,128)(2,1)S(1)} %get-tuple-element.69), channel_id=1, source_target_pairs={{0,1},{1,2},{2,3},{3,4},{4,5},{5,6},{6,7},{7,8},{8,9},{9,10},{10,1... | collective-permute-start | bytes 153848 | tf_op jit(solution)/shard_map/ppermute | solution.py:208
  5.0 0.3 collective-permute-start.1
  5.3 0.7 slice_bitcast_fusion
  5.9 0.8 bitcast_subtract_fusion
  6.7 0.7 multiply_divide_fusion
  7.7 4.9 %reshape.657 = bf16[1825,641]{1,0:T(8,128)(2,1)} reshape(bf16[5,5,73,641]{3,2,1,0:T(8,128)(2,1)} %param.9) | data formatting | bytes 4679300 | tf_op jit(solution)/shard_map/reshape | solution.py:251
  12.6 0.1 copy.112
  12.7 0.1 reshape.681
  13.2 2.4 %pad_maximum_fusion = bf16[1,641,20,49]{1,3,2,0:T(8,128)(2,1)S(1)} fusion(bf16[1,641,20,2]{1,3,2,0:T(2,128)(2,1)S(1)} %collective-permute-done.1, bf16[1,641,20,45]{1,3,2,0:T(8,128)(2,1)} %param.8, bf16[1,641,20,2]{1,3,2,0:T(2,128)(2,1)S(1)} %collective-permute-done), kind=kLoop, calls=%fused_computation.13 | loop fusion | flops 3769080 | bytes 2512720 | tf_op jit(solution)/shard_map/concatenate | solution.py:212
  15.6 2.0 reshape.656
  17.6 8.4 %convolution_bitcast_fusion = f32[1,1825,980]{2,1,0:T(8,128)} fusion(bf16[641,980]{0,1:T(8,128)(2,1)} %reshape.656, bf16[1825,641]{1,0:T(8,128)(2,1)} %reshape.657), kind=kOutput, calls=%fused_computation.7 | convolution fusion | flops 2292857088 | bytes 10750010 | tf_op jit(solution)/shard_map/kc,mcp->mkp/dot_general | solution.py:252
  25.9 8.8 %copy.94 = f32[1,1825,980]{1,2,0:T(8,128)} copy(f32[1,1825,980]{2,1,0:T(8,128)} %convolution_bitcast_fusion) | data formatting | bytes 14308000 | tf_op jit(solution)/shard_map/kc,mcp->mkp/transpose | solution.py:252
  34.7 14.5 %reshape.658 = f32[1,5,5,73,20,49]{3,2,1,5,4,0:T(8,128)} reshape(f32[1,1825,980]{1,2,0:T(8,128)} %copy.94) | data formatting | bytes 14308000 | tf_op jit(solution)/shard_map/reshape | solution.py:255
  49.2 22.3 %fusion.76 = (f32[1,1,1,73,16,45]{3,2,1,5,4,0:T(1,128)S(1)}, f32[1,1,1,73,16,45]{3,2,1,5,4,0:T(1,128)S(1)}, f32[1,1,1,73,16,45]{3,2,1,5,4,0:T(1,128)S(1)}, f32[1...) fusion(f32[1,5,5,73,20,49]{3,2,1,5,4,0:T(8,128)} %reshape.658), kind=kLoop, calls=%fused_computation.134 | loop fusion | bytes 7989120 | tf_op jit(solution)/shard_map/slice | solution.py:263
  71.5 9.1 %fusion.77 = (f32[1,1,1,73,16,45]{3,2,1,5,4,0:T(1,128)S(1)}, f32[1,1,1,73,16,45]{3,2,1,5,4,0:T(1,128)S(1)}, f32[1,1,1,73,16,45]{3,2,1,5,4,0:T(1,128)S(1)}, f32[1...) fusion(f32[1,5,5,73,20,49]{3,2,1,5,4,0:T(8,128)} %reshape.658), kind=kLoop, calls=%fused_computation.135 | loop fusion | bytes 2522880 | tf_op jit(solution)/shard_map/slice | solution.py:263
  80.7 3.6 %add_convert_fusion = bf16[1,73,8,90]{1,0,3,2:T(2,128)(2,1)S(1)} fusion(f32[1,73,8,90]{1,0,3,2:T(1,128)S(1)} %bitcast.220, f32[1,73,8,90]{1,0,3,2:T(1,128)S(1)} %bitcast.221, f32[1,73,8,90]{1,0,3,2:T(1,128)S(1)} %bitcast.222, f32[1,73,8,90]{1,0,3,2:T(1,128)S(1)} %bitcast.223, f32[1,73,8,90]{1,0,3,2:T(1,128)S(1)} %bitcast.224, ...), kind=kLoop, calls=%fused_computation.44 | loop fusion | flops 1366560 | bytes 5361412 | tf_op jit(solution)/shard_map/convert_element_type | solution.py:272
  84.3 1.0 copy.95
  85.3 4.8 %all-to-all-start = ((bf16[1,73,8,90]{3,1,0,2:T(8,128)(2,1)}), bf16[1,73,8,90]{3,1,0,2:T(8,128)(2,1)S(1)}, u32[]{:S(2)}, u32[]{:S(2)}) async-start(bf16[1,73,8,90]{3,1,0,2:T(8,128)(2,1)} %copy.95), calls=%async_computation | async-start | bytes 327680 | tf_op jit(solution)/shard_map/all_to_all | solution.py:284
  90.1 5.7 %all-to-all-done = bf16[1,73,8,90]{3,1,0,2:T(8,128)(2,1)S(1)} async-done(((bf16[1,73,8,90]{3,1,0,2:T(8,128)(2,1)}), bf16[1,73,8,90]{3,1,0,2:T(8,128)(2,1)S(1)}, u32[]{:S(2)}, u32[]{:S(2)}) %all-to-all-start) | async-done | bytes 105152 | tf_op jit(solution)/shard_map/all_to_all | solution.py:284
  95.9 1.5 fusion.7
  97.4 0.2 fusion.19
  97.7 0.6 gather_fusion
  98.4 0.6 copy.106
  99.0 3.3 %all-to-all-start.2 = ((f32[8,1,270]{2,1,0:T(1,128)}), f32[8,1,270]{2,1,0:T(1,128)S(1)}, u32[]{:S(2)}, u32[]{:S(2)}) async-start(f32[8,1,270]{2,1,0:T(1,128)} %copy.106), calls=%async_computation.2 | async-start | bytes 24576 | tf_op jit(solution)/shard_map/all_to_all | solution.py:301
  102.3 0.2 fusion.14
  102.5 0.7 copy.102
  103.2 4.1 %all-to-all-done.2 = f32[8,1,270]{2,1,0:T(1,128)S(1)} async-done(((f32[8,1,270]{2,1,0:T(1,128)}), f32[8,1,270]{2,1,0:T(1,128)S(1)}, u32[]{:S(2)}, u32[]{:S(2)}) %all-to-all-start.2) | async-done | bytes 8672 | tf_op jit(solution)/shard_map/all_to_all | solution.py:301
  107.3 3.4 %all-to-all-start.1 = ((bf16[8,73,1,90]{3,1,2,0:T(8,128)(2,1)}), bf16[8,73,1,90]{3,1,2,0:T(8,128)(2,1)S(1)}, u32[]{:S(2)}, u32[]{:S(2)}) async-start(bf16[8,73,1,90]{3,1,2,0:T(8,128)(2,1)} %copy.102), calls=%async_computation.1 | async-start | bytes 327680 | tf_op jit(solution)/shard_map/all_to_all | solution.py:290
  110.7 0.6 reshape.660
  111.3 5.0 %all-to-all-done.1 = bf16[8,73,1,90]{3,1,2,0:T(8,128)(2,1)S(1)} async-done(((bf16[8,73,1,90]{3,1,2,0:T(8,128)(2,1)}), bf16[8,73,1,90]{3,1,2,0:T(8,128)(2,1)S(1)}, u32[]{:S(2)}, u32[]{:S(2)}) %all-to-all-start.1) | async-done | bytes 105152 | tf_op jit(solution)/shard_map/all_to_all | solution.py:290
  116.3 0.6 convert_reduce_fusion
  116.9 0.2 copy.104
  117.3 0.1 fusion.23
  117.4 0.1 fusion.25
  117.5 0.1 fusion.27
  117.6 0.1 fusion.29
  117.8 0.1 fusion.33
  117.9 0.1 fusion.35
  118.0 0.1 fusion.37
  118.1 0.1 fusion.39
  118.4 0.1 fusion.45
  118.5 0.1 fusion.47
  118.6 0.1 fusion.49
  118.8 0.1 fusion.53
  118.9 0.1 fusion.55
  119.0 0.1 fusion.57
  119.1 0.1 fusion.59
  119.3 0.1 fusion.63
  119.4 0.1 fusion.65
  119.5 0.1 fusion.67
  119.6 0.1 fusion.69
  119.7 4.9 %fusion.2 = bf16[25,73,641]{2,1,0:T(8,128)(2,1)S(1)} fusion(bf16[1,25,73,20,49]{2,4,3,1,0:T(8,128)(2,1)S(1)} %fusion.69, bf16[1,641,20,2]{1,3,2,0:T(2,128)(2,1)S(1)} %collective-permute-done.1, bf16[1,641,20,45]{1,3,2,0:T(8,128)(2,1)S(1)} %copy-done.2, bf16[1,641,20,2]{1,3,2,0:T(2,128)(2,1)S(1)} %collective-permute-done), kind=kOutput, calls=%fused_computation.8 | convolution fusion | flops 2296626176 | bytes 7173010 | tf_op jit(solution)/shard_map/dot_general | solution.py:309
  124.7 2.0 pad.20
  126.7 0.1 broadcast.243
  126.8 4.8 %scatter.4 = bf16[25,80,768]{2,1,0:T(8,128)(2,1)} dynamic-update-slice(bf16[25,80,768]{2,1,0:T(8,128)(2,1)} %pad.20, bf16[25,80,1]{2,1,0:T(8,128)(2,1)S(1)} %broadcast.243, s32[]{:T(128)} %constant.75.clone.1, s32[]{:T(128)} %constant.75.clone.1, s32[]{:T(128)} %constant.89.clone.1) | dynamic-update-slice | bytes 8004 | tf_op jit(solution)/shard_map/scatter | solution.py:317
  131.6 4.6 %copy.107 = bf16[2000,768]{0,1:T(8,128)(2,1)} copy(bf16[2000,768]{1,0:T(8,128)(2,1)} %bitcast.211) | data formatting | bytes 6144000 | tf_op jit(solution)/shard_map/reshape | solution.py:318
  136.2 4.0 %pad.22 = bf16[2048,768]{0,1:T(8,128)(2,1)} pad(bf16[2000,768]{0,1:T(8,128)(2,1)} %copy.107, bf16[]{:T(256)} %constant.88.clone.1), padding=0_48x0_0 | pad | bytes 6217730 | tf_op jit(solution)/shard_map/jit(_pad)/pad | solution.py:318
  140.2 4.6 %copy.108 = bf16[2048,2,3,128]{3,0,2,1:T(8,128)(2,1)} copy(bf16[2048,2,3,128]{0,3,2,1:T(8,128)(2,1)} %bitcast.207) | data formatting | bytes 6291456 | tf_op jit(solution)/shard_map/reshape | solution.py:319
  144.9 60.5 %shard_map.93 = bf16[2048,768]{1,0:T(8,128)(2,1)S(1)} custom-call(bf16[2,3,2048,128]{3,2,1,0:T(8,128)(2,1)} %bitcast.208), custom_call_target="tpu_custom_call" | custom-call | flops 6291456 | bytes 8388608 | tf_op jit(solution)/shard_map/pallas_call | solution.py:187
  205.4 0.2 slice.254
  205.6 3.4 %convert_multiply_fusion = f32[25,73,641]{2,1,0:T(8,128)} fusion(bf16[25,80,768]{2,1,0:T(8,128)(2,1)S(1)} %bitcast.209), kind=kLoop, calls=%fused_computation.3 | loop fusion | flops 2339650 | bytes 7018950 | tf_op jit(solution)/shard_map/mul | solution.py:324
  209.1 0.7 copy.110
  209.9 0.6 copy.115
  (37 shorter events, 1.6 us)
Async XLA Ops:
  0.6 7.0 %copy-start = (f32[73,16,45]{0,1,2:T(8,128)S(1)}, f32[73,16,45]{0,1,2:T(8,128)}, u32[]{:S(2)}) copy-start(f32[73,16,45]{0,1,2:T(8,128)} %param.11) | copy-start | bytes 630724
  1.9 11.3 %collective-permute-start = (bf16[1,641,20,2]{1,3,2,0:T(2,128)(2,1)S(1)}, bf16[1,641,20,2]{1,3,2,0:T(2,128)(2,1)S(1)}, u32[]{:S(2)}, u32[]{:S(2)}) collective-permute-start(bf16[1,641,20,2]{1,3,2,0:T(2,128)(2,1)S(1)} %get-tuple-element.69), channel_id=1, source_target_pairs={{0,1},{1,2},{2,3},{3,4},{4,5},{5,6},{6,7},{7,8},{8,9},{9,10},{10,1... | collective-permute-start | bytes 153848 | tf_op jit(solution)/shard_map/ppermute | solution.py:208
  5.0 8.2 %collective-permute-start.1 = (bf16[1,641,20,2]{1,3,2,0:T(2,128)(2,1)S(1)}, bf16[1,641,20,2]{1,3,2,0:T(2,128)(2,1)S(1)}, u32[]{:S(2)}, u32[]{:S(2)}) collective-permute-start(bf16[1,641,20,2]{1,3,2,0:T(2,128)(2,1)S(1)} %get-tuple-element.70), channel_id=1, source_target_pairs={{1,0},{2,1},{3,2},{4,3},{5,4},{6,5},{7,6},{8,7},{9,8},{10,9},{11,1... | collective-permute-start | bytes 153848 | tf_op jit(solution)/shard_map/ppermute | solution.py:211
  49.2 31.5 %copy-start.3 = (f32[73]{0:T(128)S(1)}, f32[73]{0:T(128)}, u32[]{:S(2)}) copy-start(f32[73]{0:T(128)} %param.10) | copy-start | bytes 880
  85.3 10.5 %all-to-all-start = ((bf16[1,73,8,90]{3,1,0,2:T(8,128)(2,1)}), bf16[1,73,8,90]{3,1,0,2:T(8,128)(2,1)S(1)}, u32[]{:S(2)}, u32[]{:S(2)}) async-start(bf16[1,73,8,90]{3,1,0,2:T(8,128)(2,1)} %copy.95), calls=%async_computation | async-start | bytes 327680 | tf_op jit(solution)/shard_map/all_to_all | solution.py:284
  99.0 8.3 %all-to-all-start.2 = ((f32[8,1,270]{2,1,0:T(1,128)}), f32[8,1,270]{2,1,0:T(1,128)S(1)}, u32[]{:S(2)}, u32[]{:S(2)}) async-start(f32[8,1,270]{2,1,0:T(1,128)} %copy.106), calls=%async_computation.2 | async-start | bytes 24576 | tf_op jit(solution)/shard_map/all_to_all | solution.py:301
  102.3 17.4 %copy-start.2 = (bf16[1,641,20,45]{1,3,2,0:T(8,128)(2,1)S(1)}, bf16[1,641,20,45]{1,3,2,0:T(8,128)(2,1)}, u32[]{:S(2)}) copy-start(bf16[1,641,20,45]{1,3,2,0:T(8,128)(2,1)} %param.8) | copy-start | bytes 3461404
  107.3 9.0 %all-to-all-start.1 = ((bf16[8,73,1,90]{3,1,2,0:T(8,128)(2,1)}), bf16[8,73,1,90]{3,1,2,0:T(8,128)(2,1)S(1)}, u32[]{:S(2)}, u32[]{:S(2)}) async-start(bf16[8,73,1,90]{3,1,2,0:T(8,128)(2,1)} %copy.102), calls=%async_computation.1 | async-start | bytes 327680 | tf_op jit(solution)/shard_map/all_to_all | solution.py:290
  144.9 65.6 %copy-start.1 = (f32[73,16,45]{0,1,2:T(8,128)S(1)}, f32[73,16,45]{0,1,2:T(8,128)}, u32[]{:S(2)}) copy-start(f32[73,16,45]{0,1,2:T(8,128)} %param.11) | copy-start | bytes 630724

commit v2 on v1

v2 whole, which is shorter than its diff:
```python
import math

import jax
import jax.numpy as jnp
import numpy as np
from jax import lax
from jax.experimental import pallas as pl
from jax.experimental.pallas import tpu as pltpu
from jax.sharding import PartitionSpec as P

MESH = pl.DeviceIdType.MESH
MEMBERS = 8
GROUPS = 32
TAPS = 5
CIN = 641
COUT = 73
CHAN = 80
LAT = 16
LON_DEV = 45
PITCH = 48
POINTS = LAT * PITCH
CHUNK = 2 * PITCH
CAP = 6
TAP_ROWS = TAPS * CHAN
NT = (((1,), (1,)), ((), ()))
ROWS = 2048
LANES = 128
PARTS = 3
COLS = 2 * PARTS * LANES
ORDERS = (("x", "y", "z"), ("y", "x", "z"), ("z", "x", "y"))


def position():
    member = lax.axis_index("member")
    lon = lax.axis_index("lon")
    return {
        "x": (lon // 16) * 2 + member % 2,
        "y": member // 2,
        "z": (lon // 2) % 8,
        "core": lon % 2,
    }


EXTENT = {"x": 4, "y": 4, "z": 8, "core": 2}


def device(at):
    return (at["y"] * 2 + at["x"] % 2, (at["x"] // 2) * 16 + at["z"] * 2 + at["core"])


def moved(at, axis, delta):
    there = dict(at)
    there[axis] = lax.rem(at[axis] + delta, EXTENT[axis])
    return there


def send(src, dst, send_sem, recv_sem, at):
    copy = pltpu.make_async_remote_copy(
        src_ref=src, dst_ref=dst, send_sem=send_sem, recv_sem=recv_sem,
        device_id=device(at), device_id_type=MESH,
    )
    copy.start()


def send_to(src, dst, send_sem, recv_sem, there):
    copy = pltpu.make_async_remote_copy(
        src_ref=src, dst_ref=dst, send_sem=send_sem, recv_sem=recv_sem,
        device_id=there, device_id_type=MESH,
    )
    copy.start()


def finish(ref, send_sem, recv_sem, at):
    copy = pltpu.make_async_remote_copy(
        src_ref=ref, dst_ref=ref, send_sem=send_sem, recv_sem=recv_sem,
        device_id=device(at), device_id_type=MESH,
    )
    return copy


def greet(at):
    barrier = pltpu.get_barrier_semaphore()
    count = 0
    for axis in ("core", "x", "y", "z"):
        for delta in range(1, EXTENT[axis]):
            pl.semaphore_signal(
                barrier, inc=1, device_id=device(moved(at, axis, delta)), device_id_type=MESH
            )
            count += 1
    member, lon = lax.axis_index("member"), lax.axis_index("lon")
    for delta in range(1, MEMBERS):
        there = (lax.rem(member + delta, MEMBERS), lon)
        pl.semaphore_signal(barrier, inc=1, device_id=there, device_id_type=MESH)
        count += 1
    for delta in (1, GROUPS - 1):
        there = (member, lax.rem(lon + delta, GROUPS))
        pl.semaphore_signal(barrier, inc=1, device_id=there, device_id_type=MESH)
        count += 1
    return barrier, count


def stage_rows(order):
    rows, sizes = ROWS, []
    for axis in order:
        rows //= EXTENT[axis]
        sizes.append(rows)
    return sizes


def send_halves(at, theirs, core_rx, send_sems, recv_sems):
    partner = moved(at, "core", 1)
    for k in range(PARTS):
        send(theirs.at[k], core_rx.at[k], send_sems.at[k, 0], recv_sems.at[k, 0], partner)


def all_reduce(at, mine, out, core_rx, cur, rxs, send_sems, recv_sems):
    core = at["core"]
    partner = moved(at, "core", 1)
    row = [0] * PARTS
    sizes = [stage_rows(order) for order in ORDERS]

    def launch(k, s):
        axis, rows = ORDERS[k][s], sizes[k][s]
        for delta in range(1, EXTENT[axis]):
            there = moved(at, axis, delta)
            source = cur[k][s].at[pl.ds(pl.multiple_of(there[axis] * rows, 16), rows)]
            send(source, rxs[k][s].at[delta - 1], send_sems.at[k, s + 1], recv_sems.at[k, s + 1], there)

    for k in range(PARTS):
        finish(core_rx.at[k], send_sems.at[k, 0], recv_sems.at[k, 0], partner).wait_recv()
        step = 256

        def add(i, _, k=k):
            here = pl.ds(pl.multiple_of(i * step, step), step)
            total = mine[k, here, :] + core_rx[k, here, :].astype(jnp.float32)
            cur[k][0][here, :] = total.astype(jnp.bfloat16)
            return 0

        lax.fori_loop(0, ROWS // step, add, 0)
        launch(k, 0)
    for s in range(3):
        for k in range(PARTS):
            axis, rows = ORDERS[k][s], sizes[k][s]
            finish(rxs[k][s], send_sems.at[k, s + 1], recv_sems.at[k, s + 1], partner).wait_recv()
            row[k] = row[k] + at[axis] * rows
            base = pl.multiple_of(at[axis] * rows, 16)
            step = min(rows, 128)
            lane = pl.ds(pl.multiple_of(core * (PARTS * LANES) + k * LANES, LANES), LANES)

            def add(i, _, k=k, s=s, axis=axis, base=base, step=step, lane=lane):
                total = cur[k][s][pl.ds(pl.multiple_of(base + i * step, 16), step), :].astype(jnp.float32)
                here = pl.ds(pl.multiple_of(i * step, 16), step)
                for slot in range(EXTENT[axis] - 1):
                    total = total + rxs[k][s][slot, here, :].astype(jnp.float32)
                if s < 2:
                    cur[k][s + 1][here, :] = total.astype(jnp.bfloat16)
                else:
                    out[pl.ds(pl.multiple_of(row[k], 16), step), lane] = total.astype(jnp.bfloat16)
                return 0

            if rows == step:
                add(0, 0)
            else:
                lax.fori_loop(0, rows // step, add, 0)
            if s < 2:
                launch(k, s + 1)
            else:
                gather(at, out, k, 2, row, sizes, send_sems, recv_sems)
    for s in (2, 1, 0):
        for k in range(PARTS):
            axis, rows = ORDERS[k][s], sizes[k][s]
            whole = rxs[k][s]
            finish(whole, send_sems.at[k, 4 + s], recv_sems.at[k, 4 + s], partner).wait_recv()
            row[k] = row[k] - at[axis] * rows
            if s > 0:
                gather(at, out, k, s - 1, row, sizes, send_sems, recv_sems)
            else:
                lane = pl.ds(pl.multiple_of(core * (PARTS * LANES) + k * LANES, LANES), LANES)
                send(out.at[:, lane], out.at[:, lane], send_sems.at[k, 7], recv_sems.at[k, 7], partner)
    for k in range(PARTS):
        finish(core_rx.at[k], send_sems.at[k, 7], recv_sems.at[k, 7], partner).wait_recv()
    for k in range(PARTS):
        finish(core_rx.at[k], send_sems.at[k, 0], recv_sems.at[k, 0], partner).wait_send()
        finish(core_rx.at[k], send_sems.at[k, 7], recv_sems.at[k, 7], partner).wait_send()
        for s in range(3):
            finish(rxs[k][s], send_sems.at[k, s + 1], recv_sems.at[k, s + 1], partner).wait_send()
            finish(rxs[k][s], send_sems.at[k, s + 4], recv_sems.at[k, s + 4], partner).wait_send()


def gather(at, out, k, s, row, sizes, send_sems, recv_sems):
    axis, rows = ORDERS[k][s], sizes[k][s]
    lane = pl.ds(pl.multiple_of(at["core"] * (PARTS * LANES) + k * LANES, LANES), LANES)
    block = out.at[pl.ds(pl.multiple_of(row[k], 16), rows), lane]
    for delta in range(1, EXTENT[axis]):
        send(block, block, send_sems.at[k, 4 + s], recv_sems.at[k, 4 + s], moved(at, axis, delta))


def reduce_scratch():
    shapes = [pltpu.VMEM((PARTS, ROWS, LANES), jnp.bfloat16)]
    for order in ORDERS:
        rows = ROWS
        for size in stage_rows(order):
            shapes.append(pltpu.VMEM((rows, LANES), jnp.bfloat16))
            rows = size
    for order in ORDERS:
        for axis, size in zip(order, stage_rows(order)):
            shapes.append(pltpu.VMEM((EXTENT[axis] - 1, size, LANES), jnp.bfloat16))
    shapes += [pltpu.SemaphoreType.DMA((PARTS, 8)), pltpu.SemaphoreType.DMA((PARTS, 8))]
    return shapes


def edge_picks():
    picks = np.zeros((2, PITCH, (LAT + 4) * PITCH), np.float32)
    for side, first in ((0, LON_DEV - 2), (1, 0)):
        for i in range(LAT + 4):
            for h in range(2):
                picks[side, 2 * i + h, i * PITCH + first + h] = 1.0
    return picks.reshape(2 * PITCH, -1)


def margin_places():
    places = np.zeros((TAPS, 2, LAT, 2, LAT, PITCH), np.float32)
    for b in range(TAPS):
        for side, first in ((0, -2), (1, LON_DEV)):
            for h in range(2):
                j = first + h - b + 2
                if 0 <= j < LON_DEV:
                    for i in range(LAT):
                        places[b, side, i, h, i, j] = 1.0
    return places.reshape(TAPS, 4 * LAT, POINTS)


def stage_weight(w, staged):
    zeros = jnp.zeros((16, COLS), jnp.bfloat16)
    for a in range(TAPS):
        for b in range(TAPS):
            base = (a * TAPS + b) * CHAN
            staged[base + 64 : base + 80, :] = zeros
            staged[base : base + 64, 640:COLS] = jnp.zeros((64, COLS - 640), jnp.bfloat16)
            staged[base : base + COUT, 0:CIN] = w[a, b]


def forward_own(x, staged, taps):
    for n in range(3):
        lanes = slice(n * 256, n * 256 + 256)

        def one(a, total, n=n):
            rows = pl.ds(pl.multiple_of(a * PITCH + n * 256, 16), 256)
            left = staged[pl.ds(pl.multiple_of(a * TAP_ROWS, 16), TAP_ROWS), :]
            return total + lax.dot_general(left, x[rows, :], NT, preferred_element_type=jnp.float32)

        taps[:, lanes] = lax.fori_loop(0, TAPS, one, jnp.zeros((TAP_ROWS, 256), jnp.float32))


def stage_margin(halo, margin):
    left = halo[0].astype(jnp.float32)
    right = halo[1].astype(jnp.float32)
    for a in range(TAPS):
        margin[a, 0:32, :] = left[2 * a : 2 * a + 32, :].astype(jnp.bfloat16)
        margin[a, 32:64, :] = right[2 * a : 2 * a + 32, :].astype(jnp.bfloat16)


def forward_margin(margin, staged, edge_taps):
    def one(a, total):
        left = staged[pl.ds(pl.multiple_of(a * TAP_ROWS, 16), TAP_ROWS), :]
        return total + lax.dot_general(left, margin[a], NT, preferred_element_type=jnp.float32)

    edge_taps[...] = lax.fori_loop(0, TAPS, one, jnp.zeros((TAP_ROWS, 64), jnp.float32))


def convolved(taps, edge_taps, places, bias):
    total = jnp.broadcast_to(bias, (CHAN, POINTS))
    for b in range(TAPS):
        rows = slice(b * CHAN, b * CHAN + CHAN)
        part = taps[rows, :]
        total = total + (part if b == 2 else pltpu.roll(part, (2 - b) % POINTS, 1))
        if b != 2:
            total = total + jnp.dot(
                edge_taps[rows, :], places[b].astype(jnp.float32),
                precision=lax.Precision.HIGHEST, preferred_element_type=jnp.float32,
            )
    return total


def kernel_terms(values, target, vectors, gradients, score):
    lane = lax.broadcasted_iota(jnp.int32, (16, LANES), 1)
    real = (lane < LON_DEV) | ((lane >= PITCH) & (lane < PITCH + LON_DEV))

    def block(t, score_sum):
        rows = pl.ds(pl.multiple_of(t * 16, 16), 16)
        members = [values[m, rows, :].astype(jnp.float32) for m in range(MEMBERS)]
        width = vectors[rows, :][:, 1:2]
        inverse = jnp.broadcast_to(1.0 / (width * width), (16, LANES))
        half = -0.5 * inverse
        goal = target[rows, :]
        pulls = [jnp.zeros((16, LANES), jnp.float32) for _ in range(MEMBERS)]
        pair_sum = jnp.zeros((16, LANES), jnp.float32)
        for m in range(MEMBERS):
            for n in range(m + 1, MEMBERS):
                spread = members[m] - members[n]
                kernel_pair = jnp.exp(spread * spread * half)
                pair_sum = pair_sum + kernel_pair
                pull = kernel_pair * spread
                pulls[m] = pulls[m] + pull
                pulls[n] = pulls[n] - pull
        obs_sum = jnp.zeros((16, LANES), jnp.float32)
        for m in range(MEMBERS):
            misfit = members[m] - goal
            kernel_obs = jnp.exp(misfit * misfit * half)
            obs_sum = obs_sum + kernel_obs
            gradient = inverse * (misfit * kernel_obs - pulls[m] * (1.0 / MEMBERS))
            gradients[m, rows, :] = jnp.where(real, gradient, 0.0).astype(jnp.bfloat16)
        per_channel = (MEMBERS + 2.0 * pair_sum) * (1.0 / (2 * MEMBERS * MEMBERS)) - obs_sum * (1.0 / MEMBERS)
        channel = t * 16 + lax.broadcasted_iota(jnp.int32, (16, LANES), 0)
        return score_sum + jnp.where(channel < COUT, per_channel, 0.0)

    total = lax.fori_loop(0, CHAN // 16, block, jnp.zeros((16, LANES), jnp.float32))
    score[...] = jnp.broadcast_to(jnp.sum(total, axis=0, keepdims=True) * (1.0 / COUT), (8, LANES))


def stack_gradient(gathered, grad_out, stacked, edge_stacked, places):
    grad = jnp.concatenate(
        [gathered[q].astype(jnp.float32)[:, :CHUNK] for q in range(MEMBERS)], axis=1
    )
    packed = grad.astype(jnp.bfloat16)
    grad_out[...] = packed
    for b in range(TAPS):
        rows = slice(b * CHAN, b * CHAN + CHAN)
        if b == 2:
            stacked[rows, :] = packed
            edge_stacked[rows, :] = jnp.zeros((CHAN, 64), jnp.bfloat16)
        else:
            stacked[rows, :] = pltpu.roll(grad, (b - 2) % POINTS, 1).astype(jnp.bfloat16)
            edge = lax.dot_general(packed, places[b], NT, preferred_element_type=jnp.float32)
            edge_stacked[rows, :] = edge.astype(jnp.bfloat16)


def weight_terms(half, x, margin, stacked, edge_stacked, into):
    lanes = pl.ds(pl.multiple_of(half * (PARTS * LANES), LANES), PARTS * LANES)

    def one(a, _):
        right = x[pl.ds(pl.multiple_of(a * PITCH, 16), POINTS), lanes]
        total = jnp.dot(stacked[...], right, preferred_element_type=jnp.float32)
        total = total + jnp.dot(
            edge_stacked[...], margin[a, :, lanes], preferred_element_type=jnp.float32
        )
        total = total.astype(into.dtype)
        for k in range(PARTS):
            into[k, pl.ds(pl.multiple_of(a * TAP_ROWS, 16), TAP_ROWS), :] = total[
                :, k * LANES : (k + 1) * LANES
            ]
        return 0

    lax.fori_loop(0, TAPS, one, 0)
    for k in range(PARTS):
        into[k, TAPS * TAP_ROWS : ROWS, :] = jnp.zeros((ROWS - TAPS * TAP_ROWS, LANES), into.dtype)


def own_scores(starts, score_rx, owned):
    lane = lax.broadcasted_iota(jnp.int32, (8, LANES), 1)
    row = lax.broadcasted_iota(jnp.int32, (8, LANES), 0)
    me = lax.axis_index("member")
    first, count = starts[me], starts[me + 1] - starts[me]
    wanted = jnp.where(row < count, first + row, -1)
    total = jnp.zeros((8, LANES), jnp.float32)
    for q in range(MEMBERS):
        pair = score_rx[q]
        low = jnp.where(lane < LON_DEV, pair, 0.0)
        high = jnp.where(lane < LON_DEV, pltpu.roll(pair, LANES - PITCH, 1), 0.0)
        total = total + jnp.where(wanted == 2 * q, low, 0.0) + jnp.where(wanted == 2 * q + 1, high, 0.0)
    owned[...] = total


def whole_kernel(x, w, vectors, target, places, picks, starts, out, grad_out, owned, *scratch):
    (
        staged, edges, halo, margin, taps, edge_taps, to_score, values, gradients, gathered, score, score_rx,
        stacked, edge_stacked, theirs, mine, near_send, near_recv,
    ) = scratch[:18]
    core_rx, rest = scratch[18], scratch[19:]
    cur = [rest[3 * k : 3 * k + 3] for k in range(PARTS)]
    rxs = [rest[9 + 3 * k : 12 + 3 * k] for k in range(PARTS)]
    send_sems, recv_sems = rest[18], rest[19]
    at = position()
    member, lon = lax.axis_index("member"), lax.axis_index("lon")
    ahead = (member, lax.rem(lon + 1, GROUPS))
    behind = (member, lax.rem(lon + GROUPS - 1, GROUPS))
    others = [lax.rem(member + delta, MEMBERS) for delta in range(1, MEMBERS)]

    barrier, count = greet(at)
    edge = jnp.dot(picks[...], x[...], preferred_element_type=jnp.float32).astype(jnp.bfloat16)
    edges[0] = edge[:PITCH]
    edges[1] = edge[PITCH:]
    pl.semaphore_wait(barrier, count)
    send_to(edges.at[0], halo.at[0], near_send.at[0], near_recv.at[0], ahead)
    send_to(edges.at[1], halo.at[1], near_send.at[1], near_recv.at[1], behind)
    stage_weight(w, staged)
    forward_own(x, staged, taps)
    finish(halo.at[0], near_send.at[0], near_recv.at[0], at).wait()
    finish(halo.at[1], near_send.at[1], near_recv.at[1], at).wait()
    stage_margin(halo, margin)
    forward_margin(margin, staged, edge_taps)
    outputs = convolved(taps, edge_taps, places, vectors[...][:, 0:1])
    for q in range(MEMBERS):
        to_score[q, :, 0:CHUNK] = outputs[:, q * CHUNK : (q + 1) * CHUNK].astype(jnp.bfloat16)
        to_score[q, :, CHUNK:LANES] = jnp.zeros((CHAN, LANES - CHUNK), jnp.bfloat16)
    for there in others:
        send_to(to_score.at[there], values.at[member], near_send.at[2], near_recv.at[2], (there, lon))
    values[member] = to_score[member]
    finish(values.at[0:7], near_send.at[2], near_recv.at[2], at).wait_recv()
    kernel_terms(values, target, vectors, gradients, score)
    for there in others:
        send_to(gradients.at[there], gathered.at[member], near_send.at[3], near_recv.at[3], (there, lon))
    for there in others:
        send_to(score, score_rx.at[member], near_send.at[4], near_recv.at[4], (there, lon))
    gathered[member] = gradients[member]
    score_rx[member] = score[...]
    finish(gathered.at[0:7], near_send.at[3], near_recv.at[3], at).wait_recv()
    stack_gradient(gathered, grad_out, stacked, edge_stacked, places)
    weight_terms(1 - at["core"], x, margin, stacked, edge_stacked, theirs)
    send_halves(at, theirs, core_rx, send_sems, recv_sems)
    weight_terms(at["core"], x, margin, stacked, edge_stacked, mine)
    finish(score_rx.at[0:7], near_send.at[4], near_recv.at[4], at).wait_recv()
    own_scores(starts, score_rx, owned)
    all_reduce(at, mine, out, core_rx, cur, rxs, send_sems, recv_sems)
    finish(values.at[0:7], near_send.at[2], near_recv.at[2], at).wait_send()
    finish(gathered.at[0:7], near_send.at[3], near_recv.at[3], at).wait_send()
    finish(score_rx.at[0:7], near_send.at[4], near_recv.at[4], at).wait_send()


def kernel_scratch():
    chunk = (MEMBERS, CHAN, LANES)
    return [
        pltpu.VMEM((TAPS * TAP_ROWS, COLS), jnp.bfloat16),
        pltpu.VMEM((2, PITCH, COLS), jnp.bfloat16),
        pltpu.VMEM((2, PITCH, COLS), jnp.bfloat16),
        pltpu.VMEM((TAPS, 64, COLS), jnp.bfloat16),
        pltpu.VMEM((TAP_ROWS, POINTS), jnp.float32),
        pltpu.VMEM((TAP_ROWS, 64), jnp.float32),
        pltpu.VMEM(chunk, jnp.bfloat16),
        pltpu.VMEM(chunk, jnp.bfloat16),
        pltpu.VMEM(chunk, jnp.bfloat16),
        pltpu.VMEM(chunk, jnp.bfloat16),
        pltpu.VMEM((8, LANES), jnp.float32),
        pltpu.VMEM((MEMBERS, 8, LANES), jnp.float32),
        pltpu.VMEM((TAP_ROWS, POINTS), jnp.bfloat16),
        pltpu.VMEM((TAP_ROWS, 64), jnp.bfloat16),
        pltpu.VMEM((PARTS, ROWS, LANES), jnp.bfloat16),
        pltpu.VMEM((PARTS, ROWS, LANES), jnp.float32),
        pltpu.SemaphoreType.DMA((5,)),
        pltpu.SemaphoreType.DMA((5,)),
    ] + reduce_scratch()


def padded_field(fields):
    field = jnp.transpose(fields[0], (1, 2, 0))
    field = jnp.pad(field, ((0, 0), (0, PITCH - LON_DEV), (0, COLS - CIN)))
    longitude = lax.broadcasted_iota(jnp.int32, field.shape, 1)
    channel = lax.broadcasted_iota(jnp.int32, field.shape, 2)
    field = jnp.where((channel == CIN) & (longitude < LON_DEV), jnp.bfloat16(1), field)
    return field.reshape((LAT + 4) * PITCH, COLS)


def body(fields, weight, out_bias, observed, widths, owner_start):
    x = padded_field(fields)
    extra = CHAN - COUT
    vectors = jnp.stack([jnp.pad(out_bias, (0, extra)), jnp.pad(widths, (0, extra), constant_values=1.0)], axis=1)
    vectors = jnp.pad(vectors, ((0, 0), (0, LANES - 2)))
    target = lax.dynamic_slice_in_dim(observed, 2 * lax.axis_index("member"), 2, 1)
    target = jnp.pad(target, ((0, extra), (0, 0), (0, PITCH - LON_DEV))).reshape(CHAN, CHUNK)
    target = jnp.pad(target, ((0, 0), (0, LANES - CHUNK)))
    vmem = pl.BlockSpec(memory_space=pltpu.VMEM)
    summed, grad, owned = pl.pallas_call(
        whole_kernel,
        out_shape=[
            jax.ShapeDtypeStruct((ROWS, COLS), jnp.bfloat16),
            jax.ShapeDtypeStruct((CHAN, POINTS), jnp.bfloat16),
            jax.ShapeDtypeStruct((8, LANES), jnp.float32),
        ],
        in_specs=[vmem] * 6 + [pl.BlockSpec(memory_space=pltpu.SMEM)],
        out_specs=[vmem] * 3,
        scratch_shapes=kernel_scratch(),
        compiler_params=pltpu.CompilerParams(
            collective_id=1, has_side_effects=True, vmem_limit_bytes=56 * 1024 * 1024
        ),
        cost_estimate=pl.CostEstimate(flops=6 << 30, bytes_accessed=16 << 20, transcendentals=1 << 20),
    )(
        x, weight, vectors, target, jnp.asarray(margin_places(), jnp.bfloat16),
        jnp.asarray(edge_picks(), jnp.bfloat16), owner_start[0],
    )
    factor = 1.0 / math.sqrt(MEMBERS * LAT * LON_DEV * GROUPS)
    summed = summed[: TAPS * TAP_ROWS].reshape(TAPS, TAPS, CHAN, COLS)
    weight_grad = summed[:, :, :COUT, :CIN].astype(jnp.float32) * factor
    bias_grad = summed[2, 2, :COUT, CIN].astype(jnp.float32) * factor
    out_grad = grad.reshape(CHAN, LAT, PITCH)[None, :COUT, :, :LON_DEV]
    owned_score = owned[:CAP, :LON_DEV].reshape(1, 1, CAP * LON_DEV)
    return (out_grad, owned_score, weight_grad, bias_grad)


def solution(mesh):
    in_specs = (P("member", None, None, "lon"), P(), P(), P(None, None, "lon"), P(), P("lon", None))
    out_specs = (P("member", None, None, "lon"), P("lon", "member", None), P(), P())
    return jax.shard_map(body, mesh=mesh, in_specs=in_specs, out_specs=out_specs, check_vma=False)
```

time: 212 us -> 97.4 us (0.46)
  local copies, waits for them, and re-layouts: 92.3 us -> 6.74 us
  Pallas kernels: 60.5 us -> 82.7 us
  starting transfers between devices: 14.9 us -> 0 us
  waiting for transfers between devices: 14.8 us -> 0 us
  matrix products: 13.3 us -> 0 us
  other arithmetic: 13.8 us -> 7.04 us
    slice x5 -> x1, local copies, waits for them, and re-layouts: 33.5 us -> 2.07 us  [body(): summed = summed[:TAPS * TAP_ROWS].reshape(TAPS, TAPS, CHAN, COLS)]
    reshape x6 -> x2, local copies, waits for them, and re-layouts: 29.3 us -> 0.72 us  [the longest x1 0.64 us: body(): owned_score = owned[:CAP, :LON_DEV].reshape(1, 1, CAP * LON_DEV)]
    pallas_call x1, Pallas kernels: 60.5 us -> 82.7 us  [body(): pl.pallas_call(whole_kernel, out_shape=[jax.ShapeDtypeStruct((ROWS, COLS)...]
    all_to_all x3 -> x0, waiting for transfers between devices: 14.7 us -> none  [the longest x1 5.67 us: body(): lax.all_to_all(sending, 'member', split_axis=2, concat_axis=0, tiled=True)]
    dot_general x2 -> x0, matrix products: 13.3 us -> none  [the longest x1 8.36 us: body(): jnp.einsum('kc,mcp->mkp', flat_weight, flat_field, preferred_element_type...]
    all_to_all x3 -> x0, starting transfers between devices: 11.5 us -> none  [the longest x1 4.82 us: body(): lax.all_to_all(sending, 'member', split_axis=2, concat_axis=0, tiled=True)]
    transpose x1 -> x0, local copies, waits for them, and re-layouts: 8.75 us -> none  [body(): jnp.einsum('kc,mcp->mkp', flat_weight, flat_field, preferred_element_type...]
    scatter x1 -> x0, local copies, waits for them, and re-layouts: 4.78 us -> none  [body(): terms = terms.at[:, :, in_chan].set(bias_column[None])]
  transfers between devices with their start and end apart: 5 -> 0, of which waited for: 3 -> 0; matrix products, arithmetic and copies ran while one was open for 4% -> 0% of each run, Pallas kernels for 0% -> 0%
where the time goes in v2:
time: 97.4 us; the launch traced here: 97.2 us
  Pallas kernels  82.7 us (85%)
  other arithmetic  7.04 us (7%)
  local copies, waits for them, and re-layouts  6.74 us (7%)
    pallas_call x1, Pallas kernels, body(): pl.pallas_call(whole_kernel, out_shape=[jax.ShapeDtypeStruct((ROWS, COLS)...  82.7 us
    mul x1, other arithmetic, body(): weight_grad = summed[:, :, :COUT, :CIN].astype(jnp.float32) * factor  3.44 us
    select_n x1, other arithmetic, padded_field(): jnp.where((channel == CIN) & (longitude < LON_DEV), jnp.bfloat16(1), field)  2.88 us
    slice x1, local copies, waits for them, and re-layouts, body(): summed = summed[:TAPS * TAP_ROWS].reshape(TAPS, TAPS, CHAN, COLS)  2.07 us

profile of v2, /device:TPU:1, one launch (start us, length us, event | category | flops | bytes accessed | tf_op | source)
XLA Modules:
  0.0 97.2 jit_solution(14911207603831166086)
XLA Ops:
  0.6 0.0 copy-start
  0.7 1.0 %copy-done = f32[73,16,45]{0,1,2:T(8,128)S(1)} copy-done((f32[73,16,45]{0,1,2:T(8,128)S(1)}, f32[73,16,45]{0,1,2:T(8,128)}, u32[]{:S(2)}) %copy-start) | copy-done | bytes 210264
  1.7 0.1 copy.24
  1.8 0.6 pad.29.target
  2.4 0.7 pad_bitcast_fusion
  3.1 0.1 copy.22
  3.2 0.6 pad.27.vectors
  3.8 2.9 %and_select_fusion = bf16[20,48,768]{2,1,0:T(8,128)(2,1)} fusion(bf16[20,45,641]{2,1,0:T(8,128)(2,1)} %bitcast.17, pred[768]{0:T(1024)(128)(4,1)S(1)} %iota_compare_fusion, pred[48]{0:T(512)(128)(4,1)S(1)} %iota_compare_fusion.1), kind=kLoop, calls=%fused_computation.1 | loop fusion | flops 1474560 | bytes 2629176 | tf_op jit(solution)/shard_map/jit(_where)/select_n | solution.py:459
  6.7 82.7 %shard_map.111 = (bf16[2048,768]{1,0:T(8,128)(2,1)}, bf16[80,768]{1,0:T(8,128)(2,1)}, f32[8,128]{1,0:T(8,128)}) custom-call(bf16[960,768]{1,0:T(8,128)(2,1)} %bitcast.18, bf16[5,5,73,641]{3,2,1,0:T(8,128)(2,1)} %w.1, f32[80,128]{1,0:T(8,128)} %pad.27.vectors, f32[80,128]{1,0:T(8,128)} %pad.29.target, bf16[5,64,768]{2,1,0:T(8,128)(2,1)} %constant.31.clone.places, ...), custom_call_target="tpu_custom_call" | custom-call | flops 6442450944 | bytes 16777216 | tf_op jit(solution)/shard_map/pallas_call | solution.py:472
  89.4 2.1 %slice.17 = bf16[2000,768]{1,0:T(8,128)(2,1)S(1)} slice(bf16[2048,768]{1,0:T(8,128)(2,1)} %get-tuple-element.9), slice={[0:2000], [0:768]} | slice | bytes 6144000 | tf_op jit(solution)/shard_map/slice | solution.py:491
  91.5 0.0 copy-start.1
  91.5 0.0 copy-start.2
  91.5 3.4 %convert_multiply_fusion = f32[5,5,73,641]{3,2,1,0:T(8,128)} fusion(bf16[5,5,80,768]{3,2,1,0:T(8,128)(2,1)S(1)} %bitcast.15), kind=kLoop, calls=%fused_computation | loop fusion | flops 2339650 | bytes 7018950 | tf_op jit(solution)/shard_map/mul | solution.py:492
  95.0 0.7 multiply_reduce_fusion
  95.7 0.0 copy-done.1
  95.7 0.2 copy.25
  95.8 0.7 copy.26
  96.6 0.0 copy-done.2
  96.6 0.6 reshape.29
  (7 shorter events, 0.1 us)
Async XLA Ops:
  0.6 1.0 %copy-start = (f32[73,16,45]{0,1,2:T(8,128)S(1)}, f32[73,16,45]{0,1,2:T(8,128)}, u32[]{:S(2)}) copy-start(f32[73,16,45]{0,1,2:T(8,128)} %param.11) | copy-start | bytes 630724
  91.5 4.2 %copy-start.1 = (bf16[80,768]{1,0:T(8,128)(2,1)S(1)}, bf16[80,768]{1,0:T(8,128)(2,1)}, u32[]{:S(2)}) copy-start(bf16[80,768]{1,0:T(8,128)(2,1)} %get-tuple-element.7) | copy-start | bytes 368644
  91.5 5.1 %copy-start.2 = (f32[8,128]{1,0:T(8,128)S(1)}, f32[8,128]{1,0:T(8,128)}, u32[]{:S(2)}) copy-start(f32[8,128]{1,0:T(8,128)} %get-tuple-element.8) | copy-start | bytes 12292

commit v3 on v2

--- a/solution.py
+++ b/solution.py
@@ -113,7 +113,7 @@
         send(theirs.at[k], core_rx.at[k], send_sems.at[k, 0], recv_sems.at[k, 0], partner)
 
 
-def all_reduce(at, mine, out, core_rx, cur, rxs, send_sems, recv_sems):
+def all_reduce(at, mine, out, core_rx, cur, rxs, send_sems, recv_sems, meanwhile):
     core = at["core"]
     partner = moved(at, "core", 1)
     row = [0] * PARTS
@@ -138,6 +138,7 @@
 
         lax.fori_loop(0, ROWS // step, add, 0)
         launch(k, 0)
+    meanwhile()
     for s in range(3):
         for k in range(PARTS):
             axis, rows = ORDERS[k][s], sizes[k][s]
@@ -176,7 +177,7 @@
                 gather(at, out, k, s - 1, row, sizes, send_sems, recv_sems)
             else:
                 lane = pl.ds(pl.multiple_of(core * (PARTS * LANES) + k * LANES, LANES), LANES)
-                send(out.at[:, lane], out.at[:, lane], send_sems.at[k, 7], recv_sems.at[k, 7], partner)
+                send(out.at[0:ROWS, lane], out.at[0:ROWS, lane], send_sems.at[k, 7], recv_sems.at[k, 7], partner)
     for k in range(PARTS):
         finish(core_rx.at[k], send_sems.at[k, 7], recv_sems.at[k, 7], partner).wait_recv()
     for k in range(PARTS):
@@ -230,14 +231,67 @@
     return places.reshape(TAPS, 4 * LAT, POINTS)
 
 
+def stage_field(raw, x):
+    lane = lax.broadcasted_iota(jnp.int32, (PITCH, LANES), 1)
+    row = lax.broadcasted_iota(jnp.int32, (PITCH, LANES), 0)
+    tail = jnp.where((lane == CIN - 640) & (row < LON_DEV), 1.0, 0.0).astype(jnp.bfloat16)
+    zeros = jnp.zeros((16, COLS), jnp.bfloat16)
+
+    def one(i, _):
+        base = pl.multiple_of(i * PITCH, 16)
+        x[pl.ds(base + 32, 16), :] = zeros
+        x[pl.ds(base, PITCH), 640:COLS] = tail
+        x[pl.ds(base, LON_DEV), 0:CIN] = raw[i]
+        return 0
+
+    lax.fori_loop(0, LAT + 4, one, 0)
+
+
+def stage_columns(bias, widths, tile, vectors):
+    tile[...] = jnp.ones((8, LANES), jnp.float32)
+    tile[0:1, 0:COUT] = bias[...]
+    tile[1:2, 0:COUT] = widths[...]
+    vectors[:, 0:8] = jnp.transpose(tile[...])[0:CHAN, :]
+
+
+def stage_target(observed, wide, target):
+    spots = LON_DEV * LAT
+    point = lax.broadcasted_iota(jnp.int32, (LANES, spots), 0)
+    spot = lax.broadcasted_iota(jnp.int32, (LANES, spots), 1)
+    second = (point >= PITCH).astype(jnp.int32)
+    wanted = (point - PITCH * second) * LAT + 2 * lax.axis_index("member") + second
+    chosen = ((spot == wanted) & (point < CHUNK)).astype(jnp.float32)
+    wide[...] = jnp.zeros((LANES, LANES), jnp.float32)
+    wide[:, 0:COUT] = jnp.dot(
+        chosen, observed[...].reshape(spots, COUT),
+        precision=lax.Precision.HIGHEST, preferred_element_type=jnp.float32,
+    )
+    target[...] = jnp.transpose(wide[...])[0:CHAN, :]
+
+
+def write_gradient(packed, grad_out):
+    spots = LON_DEV * LAT
+    spot = lax.broadcasted_iota(jnp.int32, (spots, POINTS), 0)
+    point = lax.broadcasted_iota(jnp.int32, (spots, POINTS), 1)
+    wanted = (spot & (LAT - 1)) * PITCH + (spot >> 4)
+    moves = jnp.where(point == wanted, 1.0, 0.0).astype(jnp.bfloat16)
+    moved_grad = lax.dot_general(moves, packed[...], NT, preferred_element_type=jnp.float32)
+    grad_out[...] = moved_grad.astype(jnp.bfloat16).reshape(LON_DEV, LAT, CHAN)[:, :, :COUT]
+
+
 def stage_weight(w, staged):
     zeros = jnp.zeros((16, COLS), jnp.bfloat16)
-    for a in range(TAPS):
+    tail = jnp.zeros((64, COLS - 640), jnp.bfloat16)
+
+    def one(a, _):
         for b in range(TAPS):
-            base = (a * TAPS + b) * CHAN
-            staged[base + 64 : base + 80, :] = zeros
-            staged[base : base + 64, 640:COLS] = jnp.zeros((64, COLS - 640), jnp.bfloat16)
-            staged[base : base + COUT, 0:CIN] = w[a, b]
+            base = pl.multiple_of(a * TAP_ROWS + b * CHAN, 16)
+            staged[pl.ds(base + 64, 16), :] = zeros
+            staged[pl.ds(base, 64), 640:COLS] = tail
+            staged[pl.ds(base, COUT), 0:CIN] = w[a, b]
+        return 0
+
+    lax.fori_loop(0, TAPS, one, 0)
 
 
 def forward_own(x, staged, taps):
@@ -318,12 +372,12 @@
     score[...] = jnp.broadcast_to(jnp.sum(total, axis=0, keepdims=True) * (1.0 / COUT), (8, LANES))
 
 
-def stack_gradient(gathered, grad_out, stacked, edge_stacked, places):
+def stack_gradient(gathered, packed_grad, stacked, edge_stacked, places):
     grad = jnp.concatenate(
         [gathered[q].astype(jnp.float32)[:, :CHUNK] for q in range(MEMBERS)], axis=1
     )
     packed = grad.astype(jnp.bfloat16)
-    grad_out[...] = packed
+    packed_grad[...] = packed
     for b in range(TAPS):
         rows = slice(b * CHAN, b * CHAN + CHAN)
         if b == 2:
@@ -371,7 +425,11 @@
     owned[...] = total
 
 
-def whole_kernel(x, w, vectors, target, places, picks, starts, out, grad_out, owned, *scratch):
+def whole_kernel(
+    raw_hbm, w_hbm, observed_hbm, places_hbm, picks_hbm, bias, widths, starts, out, grad_out, owned, *scratch
+):
+    raw, w, observed, places, picks, x, tile, wide, vectors, target, packed, local = scratch[:12]
+    scratch = scratch[12:]
     (
         staged, edges, halo, margin, taps, edge_taps, to_score, values, gradients, gathered, score, score_rx,
         stacked, edge_stacked, theirs, mine, near_send, near_recv,
@@ -386,15 +444,31 @@
     behind = (member, lax.rem(lon + GROUPS - 1, GROUPS))
     others = [lax.rem(member + delta, MEMBERS) for delta in range(1, MEMBERS)]
 
+    loads = [
+        pltpu.make_async_copy(source, target_ref, local.at[n])
+        for n, (source, target_ref) in enumerate(
+            ((raw_hbm, raw), (picks_hbm, picks), (w_hbm, w), (places_hbm, places), (observed_hbm, observed))
+        )
+    ]
+    for load in loads:
+        load.start()
     barrier, count = greet(at)
+    stage_columns(bias, widths, tile, vectors)
+    loads[0].wait()
+    stage_field(raw, x)
+    loads[1].wait()
     edge = jnp.dot(picks[...], x[...], preferred_element_type=jnp.float32).astype(jnp.bfloat16)
     edges[0] = edge[:PITCH]
     edges[1] = edge[PITCH:]
     pl.semaphore_wait(barrier, count)
     send_to(edges.at[0], halo.at[0], near_send.at[0], near_recv.at[0], ahead)
     send_to(edges.at[1], halo.at[1], near_send.at[1], near_recv.at[1], behind)
+    loads[2].wait()
     stage_weight(w, staged)
     forward_own(x, staged, taps)
+    loads[3].wait()
+    loads[4].wait()
+    stage_target(observed, wide, target)
     finish(halo.at[0], near_send.at[0], near_recv.at[0], at).wait()
     finish(halo.at[1], near_send.at[1], near_recv.at[1], at).wait()
     stage_margin(halo, margin)
@@ -415,13 +489,17 @@
     gathered[member] = gradients[member]
     score_rx[member] = score[...]
     finish(gathered.at[0:7], near_send.at[3], near_recv.at[3], at).wait_recv()
-    stack_gradient(gathered, grad_out, stacked, edge_stacked, places)
+    stack_gradient(gathered, packed, stacked, edge_stacked, places)
     weight_terms(1 - at["core"], x, margin, stacked, edge_stacked, theirs)
     send_halves(at, theirs, core_rx, send_sems, recv_sems)
     weight_terms(at["core"], x, margin, stacked, edge_stacked, mine)
-    finish(score_rx.at[0:7], near_send.at[4], near_recv.at[4], at).wait_recv()
-    own_scores(starts, score_rx, owned)
-    all_reduce(at, mine, out, core_rx, cur, rxs, send_sems, recv_sems)
+
+    def meanwhile():
+        write_gradient(packed, grad_out)
+        finish(score_rx.at[0:7], near_send.at[4], near_recv.at[4], at).wait_recv()
+        own_scores(starts, score_rx, owned)
+
+    all_reduce(at, mine, out, core_rx, cur, rxs, send_sems, recv_sems, meanwhile)
     finish(values.at[0:7], near_send.at[2], near_recv.at[2], at).wait_send()
     finish(gathered.at[0:7], near_send.at[3], near_recv.at[3], at).wait_send()
     finish(score_rx.at[0:7], near_send.at[4], near_recv.at[4], at).wait_send()
@@ -430,6 +508,18 @@
 def kernel_scratch():
     chunk = (MEMBERS, CHAN, LANES)
     return [
+        pltpu.VMEM((LAT + 4, LON_DEV, CIN), jnp.bfloat16),
+        pltpu.VMEM((TAPS, TAPS, COUT, CIN), jnp.bfloat16),
+        pltpu.VMEM((LON_DEV, LAT, COUT), jnp.float32),
+        pltpu.VMEM((TAPS, 4 * LAT, POINTS), jnp.bfloat16),
+        pltpu.VMEM((2 * PITCH, (LAT + 4) * PITCH), jnp.bfloat16),
+        pltpu.VMEM(((LAT + 4) * PITCH, COLS), jnp.bfloat16),
+        pltpu.VMEM((8, LANES), jnp.float32),
+        pltpu.VMEM((LANES, LANES), jnp.float32),
+        pltpu.VMEM((CHAN, LANES), jnp.float32),
+        pltpu.VMEM((CHAN, LANES), jnp.float32),
+        pltpu.VMEM((CHAN, POINTS), jnp.bfloat16),
+        pltpu.SemaphoreType.DMA((5,)),
         pltpu.VMEM((TAPS * TAP_ROWS, COLS), jnp.bfloat16),
         pltpu.VMEM((2, PITCH, COLS), jnp.bfloat16),
         pltpu.VMEM((2, PITCH, COLS), jnp.bfloat16),
@@ -451,32 +541,17 @@
     ] + reduce_scratch()
 
 
-def padded_field(fields):
-    field = jnp.transpose(fields[0], (1, 2, 0))
-    field = jnp.pad(field, ((0, 0), (0, PITCH - LON_DEV), (0, COLS - CIN)))
-    longitude = lax.broadcasted_iota(jnp.int32, field.shape, 1)
-    channel = lax.broadcasted_iota(jnp.int32, field.shape, 2)
-    field = jnp.where((channel == CIN) & (longitude < LON_DEV), jnp.bfloat16(1), field)
-    return field.reshape((LAT + 4) * PITCH, COLS)
-
-
 def body(fields, weight, out_bias, observed, widths, owner_start):
-    x = padded_field(fields)
-    extra = CHAN - COUT
-    vectors = jnp.stack([jnp.pad(out_bias, (0, extra)), jnp.pad(widths, (0, extra), constant_values=1.0)], axis=1)
-    vectors = jnp.pad(vectors, ((0, 0), (0, LANES - 2)))
-    target = lax.dynamic_slice_in_dim(observed, 2 * lax.axis_index("member"), 2, 1)
-    target = jnp.pad(target, ((0, extra), (0, 0), (0, PITCH - LON_DEV))).reshape(CHAN, CHUNK)
-    target = jnp.pad(target, ((0, 0), (0, LANES - CHUNK)))
     vmem = pl.BlockSpec(memory_space=pltpu.VMEM)
+    hbm = pl.BlockSpec(memory_space=pl.ANY)
     summed, grad, owned = pl.pallas_call(
         whole_kernel,
         out_shape=[
-            jax.ShapeDtypeStruct((ROWS, COLS), jnp.bfloat16),
-            jax.ShapeDtypeStruct((CHAN, POINTS), jnp.bfloat16),
+            jax.ShapeDtypeStruct((26 * CHAN, COLS), jnp.bfloat16),
+            jax.ShapeDtypeStruct((LON_DEV, LAT, COUT), jnp.bfloat16),
             jax.ShapeDtypeStruct((8, LANES), jnp.float32),
         ],
-        in_specs=[vmem] * 6 + [pl.BlockSpec(memory_space=pltpu.SMEM)],
+        in_specs=[hbm] * 5 + [vmem] * 2 + [pl.BlockSpec(memory_space=pltpu.SMEM)],
         out_specs=[vmem] * 3,
         scratch_shapes=kernel_scratch(),
         compiler_params=pltpu.CompilerParams(
@@ -484,14 +559,15 @@
         ),
         cost_estimate=pl.CostEstimate(flops=6 << 30, bytes_accessed=16 << 20, transcendentals=1 << 20),
     )(
-        x, weight, vectors, target, jnp.asarray(margin_places(), jnp.bfloat16),
-        jnp.asarray(edge_picks(), jnp.bfloat16), owner_start[0],
+        jnp.transpose(fields[0], (1, 2, 0)), weight, jnp.transpose(observed, (2, 1, 0)),
+        jnp.asarray(margin_places(), jnp.bfloat16), jnp.asarray(edge_picks(), jnp.bfloat16),
+        out_bias.reshape(1, COUT), widths.reshape(1, COUT), owner_start[0],
     )
     factor = 1.0 / math.sqrt(MEMBERS * LAT * LON_DEV * GROUPS)
-    summed = summed[: TAPS * TAP_ROWS].reshape(TAPS, TAPS, CHAN, COLS)
-    weight_grad = summed[:, :, :COUT, :CIN].astype(jnp.float32) * factor
-    bias_grad = summed[2, 2, :COUT, CIN].astype(jnp.float32) * factor
-    out_grad = grad.reshape(CHAN, LAT, PITCH)[None, :COUT, :, :LON_DEV]
+    summed = summed.reshape(26, CHAN, COLS)
+    weight_grad = (summed[:25, :COUT, :CIN].astype(jnp.float32) * factor).reshape(TAPS, TAPS, COUT, CIN)
+    bias_grad = summed[12, :COUT, CIN].astype(jnp.float32) * factor
+    out_grad = jnp.transpose(grad, (2, 1, 0))[None]
     owned_score = owned[:CAP, :LON_DEV].reshape(1, 1, CAP * LON_DEV)
     return (out_grad, owned_score, weight_grad, bias_grad)
 

time: 97.4 us -> 91.2 us (0.936)
  local copies, waits for them, and re-layouts: 6.74 us -> 2.58 us
  Pallas kernels: 82.7 us -> 81.7 us
    select_n x1 -> x0, other arithmetic: 2.88 us -> none  [padded_field(): jnp.where((channel == CIN) & (longitude < LON_DEV), jnp.bfloat16(1), field)]
    slice x1 -> x0, local copies, waits for them, and re-layouts: 2.07 us -> none  [body(): summed = summed[:TAPS * TAP_ROWS].reshape(TAPS, TAPS, CHAN, COLS)]
    mul x2, other arithmetic: 4.14 us -> 6.15 us  [the longest x1 5.35 us: body(): summed[:25, :COUT, :CIN].astype(jnp.float32) * factor]
    pad x3 -> x0, local copies, waits for them, and re-layouts: 1.26 us -> none  [the longest x1 0.63 us: body(): target = jnp.pad(target, ((0, 0), (0, LANES - CHUNK)))]
    pallas_call x1, Pallas kernels: 82.7 us -> 81.7 us  [body(): pl.pallas_call(whole_kernel, out_shape=[jax.ShapeDtypeStruct((26 * CHAN,...]
where the time goes in v3:
time: 91.2 us; the launch traced here: 91.1 us
  Pallas kernels  81.7 us (90%)
  other arithmetic  6.15 us (7%)
  local copies, waits for them, and re-layouts  2.58 us (3%)
    pallas_call x1, Pallas kernels, body(): pl.pallas_call(whole_kernel, out_shape=[jax.ShapeDtypeStruct((26 * CHAN,...  81.7 us
    mul x1, other arithmetic, body(): summed[:25, :COUT, :CIN].astype(jnp.float32) * factor  5.35 us

profile of v3, /device:TPU:1, one launch (start us, length us, event | category | flops | bytes accessed | tf_op | source)
XLA Modules:
  0.0 91.1 jit_solution(11403910632209331742)
XLA Ops:
  0.6 81.7 %shard_map.111 = (bf16[2080,768]{1,0:T(8,128)(2,1)}, bf16[45,16,73]{2,1,0:T(8,128)(2,1)}, f32[8,128]{1,0:T(8,128)}) custom-call(bf16[20,45,641]{2,1,0:T(8,128)(2,1)} %bitcast.20, bf16[5,5,73,641]{3,2,1,0:T(8,128)(2,1)} %w_hbm.1, f32[45,16,73]{2,1,0:T(8,128)} %bitcast.21, bf16[5,64,768]{2,1,0:T(8,128)(2,1)} %constant.2.clone.places_hbm, ...), custom_call_target="tpu_custom_call" | custom-call | flops 6442450944 | bytes 16777216 | tf_op jit(solution)/shard_map/pallas_call | solution.py:547
  82.3 1.3 %reshape.28 = f32[1,1,270]{2,1,0:T(1,128)} reshape(f32[6,45]{1,0:T(8,128)} %bitcast.18) | data formatting | bytes 2160 | tf_op jit(solution)/shard_map/reshape | solution.py:571
  83.6 0.8 convert_multiply_fusion.1
  84.4 0.6 copy.14
  85.0 0.0 copy-start
  85.0 5.3 %convert_multiply_fusion = f32[25,73,641]{2,1,0:T(8,128)} fusion(bf16[26,80,768]{2,1,0:T(8,128)(2,1)} %bitcast.16), kind=kLoop, calls=%fused_computation | loop fusion | flops 2339650 | bytes 7018950 | tf_op jit(solution)/shard_map/mul | solution.py:568
  90.4 0.0 copy-done
  90.4 0.7 copy.16
Async XLA Ops:
  85.0 5.4 %copy-start = (bf16[45,16,73]{2,1,0:T(8,128)(2,1)S(1)}, bf16[45,16,73]{2,1,0:T(8,128)(2,1)}, u32[]{:S(2)}) copy-start(bf16[45,16,73]{2,1,0:T(8,128)(2,1)} %get-tuple-element.7) | copy-start | bytes 315364

commit v4 on v3

--- a/solution.py
+++ b/solution.py
@@ -26,7 +26,9 @@
 ROWS = 2048
 LANES = 128
 PARTS = 3
-COLS = 2 * PARTS * LANES
+COLS = 768
+WIDE = 640
+PART_ROWS = (2048, 2048, 1024)
 ORDERS = (("x", "y", "z"), ("y", "x", "z"), ("z", "x", "y"))
 
 
@@ -99,113 +101,134 @@
     return barrier, count
 
 
-def stage_rows(order):
-    rows, sizes = ROWS, []
-    for axis in order:
+def stage_rows(k):
+    rows, sizes = PART_ROWS[k], []
+    for axis in ORDERS[k][: 2 if k == 2 else 3]:
         rows //= EXTENT[axis]
         sizes.append(rows)
     return sizes
 
 
-def send_halves(at, theirs, core_rx, send_sems, recv_sems):
+SIZES = [stage_rows(k) for k in range(PARTS)]
+
+
+def place(at, out, k, row, rows):
+    if k == 2:
+        return out.at[pl.ds(pl.multiple_of(at["core"] * 1024 + row, 16), rows), 512:640]
+    lane = pl.multiple_of((2 * at["core"] + k) * LANES, LANES)
+    return out.at[pl.ds(pl.multiple_of(row, 16), rows), pl.ds(lane, LANES)]
+
+
+def launch(at, k, s, cur, rxs, send_sems, recv_sems):
+    axis, rows = ORDERS[k][s], SIZES[k][s]
+    for delta in range(1, EXTENT[axis]):
+        there = moved(at, axis, delta)
+        source = cur[k][s].at[pl.ds(pl.multiple_of(there[axis] * rows, 16), rows)]
+        send(source, rxs[k][s].at[delta - 1], send_sems.at[k, s + 1], recv_sems.at[k, s + 1], there)
+
+
+def add_core(at, k, mine, core_rx, cur, send_sems, recv_sems):
+    finish(core_rx[k], send_sems.at[k, 0], recv_sems.at[k, 0], at).wait_recv()
+    step = 256
+
+    def add(i, _):
+        here = pl.ds(pl.multiple_of(i * step, step), step)
+        if k == 2:
+            own = mine[pl.ds(pl.multiple_of(at["core"] * 1024 + i * step, step), step), :]
+        else:
+            own = mine[k, here, :]
+        cur[k][0][here, :] = (own + core_rx[k][here, :].astype(jnp.float32)).astype(jnp.bfloat16)
+        return 0
+
+    lax.fori_loop(0, PART_ROWS[k] // step, add, 0)
+
+
+def gather(at, out, k, s, row, send_sems, recv_sems):
+    axis = ORDERS[k][s]
+    block = place(at, out, k, row, SIZES[k][s])
+    for delta in range(1, EXTENT[axis]):
+        send(block, block, send_sems.at[k, 4 + s], recv_sems.at[k, 4 + s], moved(at, axis, delta))
+
+
+def all_reduce(at, out, core_rx, cur, rxs, shared, send_sems, recv_sems):
+    row = [0] * PARTS
     partner = moved(at, "core", 1)
-    for k in range(PARTS):
-        send(theirs.at[k], core_rx.at[k], send_sems.at[k, 0], recv_sems.at[k, 0], partner)
-
-
-def all_reduce(at, mine, out, core_rx, cur, rxs, send_sems, recv_sems, meanwhile):
-    core = at["core"]
-    partner = moved(at, "core", 1)
-    row = [0] * PARTS
-    sizes = [stage_rows(order) for order in ORDERS]
-
-    def launch(k, s):
-        axis, rows = ORDERS[k][s], sizes[k][s]
-        for delta in range(1, EXTENT[axis]):
-            there = moved(at, axis, delta)
-            source = cur[k][s].at[pl.ds(pl.multiple_of(there[axis] * rows, 16), rows)]
-            send(source, rxs[k][s].at[delta - 1], send_sems.at[k, s + 1], recv_sems.at[k, s + 1], there)
-
-    for k in range(PARTS):
-        finish(core_rx.at[k], send_sems.at[k, 0], recv_sems.at[k, 0], partner).wait_recv()
-        step = 256
-
-        def add(i, _, k=k):
-            here = pl.ds(pl.multiple_of(i * step, step), step)
-            total = mine[k, here, :] + core_rx[k, here, :].astype(jnp.float32)
-            cur[k][0][here, :] = total.astype(jnp.bfloat16)
-            return 0
-
-        lax.fori_loop(0, ROWS // step, add, 0)
-        launch(k, 0)
-    meanwhile()
     for s in range(3):
-        for k in range(PARTS):
-            axis, rows = ORDERS[k][s], sizes[k][s]
-            finish(rxs[k][s], send_sems.at[k, s + 1], recv_sems.at[k, s + 1], partner).wait_recv()
+        for k in (2, 0, 1):
+            if k == 2 and s == 2:
+                finish(shared.at[0:3], send_sems.at[k, 3], recv_sems.at[k, 3], at).wait_recv()
+                total = shared[0].astype(jnp.float32)
+                for y in range(1, 4):
+                    total = total + shared[y].astype(jnp.float32)
+                place(at, out, k, row[k], 32)[...] = total.astype(jnp.bfloat16)
+                gather(at, out, k, 1, row[k], send_sems, recv_sems)
+                continue
+            axis, rows = ORDERS[k][s], SIZES[k][s]
+            finish(rxs[k][s], send_sems.at[k, s + 1], recv_sems.at[k, s + 1], at).wait_recv()
             row[k] = row[k] + at[axis] * rows
             base = pl.multiple_of(at[axis] * rows, 16)
             step = min(rows, 128)
-            lane = pl.ds(pl.multiple_of(core * (PARTS * LANES) + k * LANES, LANES), LANES)
-
-            def add(i, _, k=k, s=s, axis=axis, base=base, step=step, lane=lane):
+
+            def add(i, _, k=k, s=s, axis=axis, base=base, step=step):
                 total = cur[k][s][pl.ds(pl.multiple_of(base + i * step, 16), step), :].astype(jnp.float32)
                 here = pl.ds(pl.multiple_of(i * step, 16), step)
                 for slot in range(EXTENT[axis] - 1):
                     total = total + rxs[k][s][slot, here, :].astype(jnp.float32)
-                if s < 2:
-                    cur[k][s + 1][here, :] = total.astype(jnp.bfloat16)
+                total = total.astype(jnp.bfloat16)
+                if k == 2 and s == 1:
+                    shared[at["y"]] = total
+                elif s == 2:
+                    place(at, out, k, row[k], step)[...] = total
                 else:
-                    out[pl.ds(pl.multiple_of(row[k], 16), step), lane] = total.astype(jnp.bfloat16)
+                    cur[k][s + 1][here, :] = total
                 return 0
 
             if rows == step:
                 add(0, 0)
             else:
                 lax.fori_loop(0, rows // step, add, 0)
-            if s < 2:
-                launch(k, s + 1)
+            if k == 2 and s == 1:
+                for delta in range(1, 4):
+                    own = shared.at[at["y"]]
+                    send(own, own, send_sems.at[k, 3], recv_sems.at[k, 3], moved(at, "y", delta))
+            elif s == 2:
+                gather(at, out, k, 2, row[k], send_sems, recv_sems)
             else:
-                gather(at, out, k, 2, row, sizes, send_sems, recv_sems)
+                launch(at, k, s + 1, cur, rxs, send_sems, recv_sems)
     for s in (2, 1, 0):
-        for k in range(PARTS):
-            axis, rows = ORDERS[k][s], sizes[k][s]
-            whole = rxs[k][s]
-            finish(whole, send_sems.at[k, 4 + s], recv_sems.at[k, 4 + s], partner).wait_recv()
+        for k in (2, 0, 1):
+            if k == 2 and s == 2:
+                continue
+            axis, rows = ORDERS[k][s], SIZES[k][s]
+            finish(rxs[k][s], send_sems.at[k, 4 + s], recv_sems.at[k, 4 + s], at).wait_recv()
             row[k] = row[k] - at[axis] * rows
             if s > 0:
-                gather(at, out, k, s - 1, row, sizes, send_sems, recv_sems)
+                gather(at, out, k, s - 1, row[k], send_sems, recv_sems)
             else:
-                lane = pl.ds(pl.multiple_of(core * (PARTS * LANES) + k * LANES, LANES), LANES)
-                send(out.at[0:ROWS, lane], out.at[0:ROWS, lane], send_sems.at[k, 7], recv_sems.at[k, 7], partner)
+                block = place(at, out, k, 0, PART_ROWS[k])
+                send(block, block, send_sems.at[k, 7], recv_sems.at[k, 7], partner)
+    for k in (2, 0, 1):
+        finish(core_rx[k], send_sems.at[k, 7], recv_sems.at[k, 7], partner).wait_recv()
     for k in range(PARTS):
-        finish(core_rx.at[k], send_sems.at[k, 7], recv_sems.at[k, 7], partner).wait_recv()
-    for k in range(PARTS):
-        finish(core_rx.at[k], send_sems.at[k, 0], recv_sems.at[k, 0], partner).wait_send()
-        finish(core_rx.at[k], send_sems.at[k, 7], recv_sems.at[k, 7], partner).wait_send()
-        for s in range(3):
+        finish(core_rx[k], send_sems.at[k, 0], recv_sems.at[k, 0], partner).wait_send()
+        finish(core_rx[k], send_sems.at[k, 7], recv_sems.at[k, 7], partner).wait_send()
+        for s in range(len(SIZES[k])):
             finish(rxs[k][s], send_sems.at[k, s + 1], recv_sems.at[k, s + 1], partner).wait_send()
             finish(rxs[k][s], send_sems.at[k, s + 4], recv_sems.at[k, s + 4], partner).wait_send()
-
-
-def gather(at, out, k, s, row, sizes, send_sems, recv_sems):
-    axis, rows = ORDERS[k][s], sizes[k][s]
-    lane = pl.ds(pl.multiple_of(at["core"] * (PARTS * LANES) + k * LANES, LANES), LANES)
-    block = out.at[pl.ds(pl.multiple_of(row[k], 16), rows), lane]
-    for delta in range(1, EXTENT[axis]):
-        send(block, block, send_sems.at[k, 4 + s], recv_sems.at[k, 4 + s], moved(at, axis, delta))
+    finish(shared.at[0:3], send_sems.at[2, 3], recv_sems.at[2, 3], partner).wait_send()
 
 
 def reduce_scratch():
-    shapes = [pltpu.VMEM((PARTS, ROWS, LANES), jnp.bfloat16)]
-    for order in ORDERS:
-        rows = ROWS
-        for size in stage_rows(order):
+    shapes = [pltpu.VMEM((PART_ROWS[k], LANES), jnp.bfloat16) for k in range(PARTS)]
+    for k in range(PARTS):
+        rows = PART_ROWS[k]
+        for size in SIZES[k]:
             shapes.append(pltpu.VMEM((rows, LANES), jnp.bfloat16))
             rows = size
-    for order in ORDERS:
-        for axis, size in zip(order, stage_rows(order)):
+    for k in range(PARTS):
+        for axis, size in zip(ORDERS[k], SIZES[k]):
             shapes.append(pltpu.VMEM((EXTENT[axis] - 1, size, LANES), jnp.bfloat16))
+    shapes.append(pltpu.VMEM((4, 32, LANES), jnp.bfloat16))
     shapes += [pltpu.SemaphoreType.DMA((PARTS, 8)), pltpu.SemaphoreType.DMA((PARTS, 8))]
     return shapes
 
@@ -389,25 +412,47 @@
             edge_stacked[rows, :] = edge.astype(jnp.bfloat16)
 
 
-def weight_terms(half, x, margin, stacked, edge_stacked, into):
-    lanes = pl.ds(pl.multiple_of(half * (PARTS * LANES), LANES), PARTS * LANES)
-
+def product(a, lanes, x, margin, stacked, edge_stacked):
+    right = x[pl.ds(pl.multiple_of(a * PITCH, 16), POINTS), lanes]
+    total = jnp.dot(stacked[...], right, preferred_element_type=jnp.float32)
+    return total + jnp.dot(edge_stacked[...], margin[a, :, lanes], preferred_element_type=jnp.float32)
+
+
+def shared_terms(x, margin, stacked, edge_stacked, fifth, fifth_sent, tails, extra):
     def one(a, _):
-        right = x[pl.ds(pl.multiple_of(a * PITCH, 16), POINTS), lanes]
-        total = jnp.dot(stacked[...], right, preferred_element_type=jnp.float32)
-        total = total + jnp.dot(
-            edge_stacked[...], margin[a, :, lanes], preferred_element_type=jnp.float32
-        )
-        total = total.astype(into.dtype)
-        for k in range(PARTS):
-            into[k, pl.ds(pl.multiple_of(a * TAP_ROWS, 16), TAP_ROWS), :] = total[
-                :, k * LANES : (k + 1) * LANES
-            ]
+        total = product(a, slice(512, 768), x, margin, stacked, edge_stacked)
+        rows = pl.ds(pl.multiple_of(a * TAP_ROWS, 16), TAP_ROWS)
+        fifth[rows, :] = total[:, :LANES]
+        fifth_sent[rows, :] = total[:, :LANES].astype(jnp.bfloat16)
+        tails[a, :, 0:TAP_ROWS] = jnp.transpose(total[:, LANES:])[0:8, :]
         return 0
 
     lax.fori_loop(0, TAPS, one, 0)
-    for k in range(PARTS):
-        into[k, TAPS * TAP_ROWS : ROWS, :] = jnp.zeros((ROWS - TAPS * TAP_ROWS, LANES), into.dtype)
+    spare = ROWS - TAPS * TAP_ROWS
+    fifth[TAPS * TAP_ROWS : ROWS, :] = jnp.zeros((spare, LANES), jnp.float32)
+    fifth_sent[TAPS * TAP_ROWS : ROWS, :] = jnp.zeros((spare, LANES), jnp.bfloat16)
+    extra[...] = jnp.zeros((16, 512), jnp.float32)
+    for a in range(TAPS):
+        extra[a : a + 1, 0:TAP_ROWS] = tails[a, 0:1, 0:TAP_ROWS]
+    extra[TAPS : TAPS + 1, 0:TAP_ROWS] = tails[2, 1:2, 0:TAP_ROWS]
+
+
+def weight_terms(half, x, margin, stacked, edge_stacked, extra, into):
+    lanes = pl.ds(pl.multiple_of(half * 256, 256), 256)
+
+    def one(a, _):
+        total = product(a, lanes, x, margin, stacked, edge_stacked).astype(into.dtype)
+        rows = pl.ds(pl.multiple_of(a * TAP_ROWS, 16), TAP_ROWS)
+        for k in range(2):
+            into[k, rows, :] = total[:, k * LANES : (k + 1) * LANES]
+        return 0
+
+    lax.fori_loop(0, TAPS, one, 0)
+    first = TAPS * TAP_ROWS
+    more = extra[:, lanes].astype(into.dtype)
+    for k in range(2):
+        into[k, first : first + 16, :] = more[:, k * LANES : (k + 1) * LANES]
+        into[k, first + 16 : ROWS, :] = jnp.zeros((ROWS - first - 16, LANES), into.dtype)
 
 
 def own_scores(starts, score_rx, owned):
@@ -432,12 +477,12 @@
     scratch = scratch[12:]
     (
         staged, edges, halo, margin, taps, edge_taps, to_score, values, gradients, gathered, score, score_rx,
-        stacked, edge_stacked, theirs, mine, near_send, near_recv,
-    ) = scratch[:18]
-    core_rx, rest = scratch[18], scratch[19:]
+        stacked, edge_stacked, theirs, mine, fifth, fifth_sent, tails, extra, near_send, near_recv,
+    ) = scratch[:22]
+    core_rx, rest = scratch[22:25], scratch[25:]
     cur = [rest[3 * k : 3 * k + 3] for k in range(PARTS)]
-    rxs = [rest[9 + 3 * k : 12 + 3 * k] for k in range(PARTS)]
-    send_sems, recv_sems = rest[18], rest[19]
+    rxs = [rest[8 + 3 * k : 11 + 3 * k] for k in range(PARTS)]
+    shared, send_sems, recv_sems = rest[16:19]
     at = position()
     member, lon = lax.axis_index("member"), lax.axis_index("lon")
     ahead = (member, lax.rem(lon + 1, GROUPS))
@@ -490,16 +535,23 @@
     score_rx[member] = score[...]
     finish(gathered.at[0:7], near_send.at[3], near_recv.at[3], at).wait_recv()
     stack_gradient(gathered, packed, stacked, edge_stacked, places)
-    weight_terms(1 - at["core"], x, margin, stacked, edge_stacked, theirs)
-    send_halves(at, theirs, core_rx, send_sems, recv_sems)
-    weight_terms(at["core"], x, margin, stacked, edge_stacked, mine)
-
-    def meanwhile():
-        write_gradient(packed, grad_out)
-        finish(score_rx.at[0:7], near_send.at[4], near_recv.at[4], at).wait_recv()
-        own_scores(starts, score_rx, owned)
-
-    all_reduce(at, mine, out, core_rx, cur, rxs, send_sems, recv_sems, meanwhile)
+    core, partner = at["core"], moved(at, "core", 1)
+    shared_terms(x, margin, stacked, edge_stacked, fifth, fifth_sent, tails, extra)
+    source = fifth_sent.at[pl.ds(pl.multiple_of((1 - core) * 1024, 16), 1024)]
+    send(source, core_rx[2], send_sems.at[2, 0], recv_sems.at[2, 0], partner)
+    weight_terms(1 - core, x, margin, stacked, edge_stacked, extra, theirs)
+    for k in range(2):
+        send(theirs.at[k], core_rx[k], send_sems.at[k, 0], recv_sems.at[k, 0], partner)
+    add_core(at, 2, fifth, core_rx, cur, send_sems, recv_sems)
+    launch(at, 2, 0, cur, rxs, send_sems, recv_sems)
+    weight_terms(core, x, margin, stacked, edge_stacked, extra, mine)
+    for k in range(2):
+        add_core(at, k, mine, core_rx, cur, send_sems, recv_sems)
+        launch(at, k, 0, cur, rxs, send_sems, recv_sems)
+    write_gradient(packed, grad_out)
+    finish(score_rx.at[0:7], near_send.at[4], near_recv.at[4], at).wait_recv()
+    own_scores(starts, score_rx, owned)
+    all_reduce(at, out, core_rx, cur, rxs, shared, send_sems, recv_sems)
     finish(values.at[0:7], near_send.at[2], near_recv.at[2], at).wait_send()
     finish(gathered.at[0:7], near_send.at[3], near_recv.at[3], at).wait_send()
     finish(score_rx.at[0:7], near_send.at[4], near_recv.at[4], at).wait_send()
@@ -534,11 +586,30 @@
         pltpu.VMEM((MEMBERS, 8, LANES), jnp.float32),
         pltpu.VMEM((TAP_ROWS, POINTS), jnp.bfloat16),
         pltpu.VMEM((TAP_ROWS, 64), jnp.bfloat16),
-        pltpu.VMEM((PARTS, ROWS, LANES), jnp.bfloat16),
-        pltpu.VMEM((PARTS, ROWS, LANES), jnp.float32),
+        pltpu.VMEM((2, ROWS, LANES), jnp.bfloat16),
+        pltpu.VMEM((2, ROWS, LANES), jnp.float32),
+        pltpu.VMEM((ROWS, LANES), jnp.float32),
+        pltpu.VMEM((ROWS, LANES), jnp.bfloat16),
+        pltpu.VMEM((TAPS, 8, 512), jnp.float32),
+        pltpu.VMEM((16, 512), jnp.float32),
         pltpu.SemaphoreType.DMA((5,)),
         pltpu.SemaphoreType.DMA((5,)),
     ] + reduce_scratch()
+
+
+def finish_kernel(main, extra, weight_grad, bias_grad):
+    factor = 1.0 / math.sqrt(MEMBERS * LAT * LON_DEV * GROUPS)
+    a = pl.program_id(0)
+    more = extra[...].astype(jnp.float32) * factor
+    number = lax.broadcasted_iota(jnp.int32, (16, WIDE), 0)
+    last = jnp.sum(jnp.where(number == a, more, 0.0), axis=0, keepdims=True)
+    last = jnp.transpose(jnp.broadcast_to(last[:, 0:512], (8, 512)))
+    for b in range(TAPS):
+        weight_grad[0, b, :, 0:WIDE] = (
+            main[b * CHAN : (b + 1) * CHAN, :].astype(jnp.float32)[:COUT, :] * factor
+        )
+        weight_grad[0, b, :, WIDE:CIN] = last[b * CHAN : b * CHAN + COUT, 0:1]
+    bias_grad[...] = more[TAPS : TAPS + 1, 2 * CHAN : 2 * CHAN + COUT]
 
 
 def body(fields, weight, out_bias, observed, widths, owner_start):
@@ -547,7 +618,7 @@
     summed, grad, owned = pl.pallas_call(
         whole_kernel,
         out_shape=[
-            jax.ShapeDtypeStruct((26 * CHAN, COLS), jnp.bfloat16),
+            jax.ShapeDtypeStruct((ROWS, WIDE), jnp.bfloat16),
             jax.ShapeDtypeStruct((LON_DEV, LAT, COUT), jnp.bfloat16),
             jax.ShapeDtypeStruct((8, LANES), jnp.float32),
         ],
@@ -563,10 +634,24 @@
         jnp.asarray(margin_places(), jnp.bfloat16), jnp.asarray(edge_picks(), jnp.bfloat16),
         out_bias.reshape(1, COUT), widths.reshape(1, COUT), owner_start[0],
     )
-    factor = 1.0 / math.sqrt(MEMBERS * LAT * LON_DEV * GROUPS)
-    summed = summed.reshape(26, CHAN, COLS)
-    weight_grad = (summed[:25, :COUT, :CIN].astype(jnp.float32) * factor).reshape(TAPS, TAPS, COUT, CIN)
-    bias_grad = summed[12, :COUT, CIN].astype(jnp.float32) * factor
+    weight_grad, bias_grad = pl.pallas_call(
+        finish_kernel,
+        grid=(TAPS,),
+        out_shape=[
+            jax.ShapeDtypeStruct((TAPS, TAPS, COUT, CIN), jnp.float32),
+            jax.ShapeDtypeStruct((1, COUT), jnp.float32),
+        ],
+        in_specs=[
+            pl.BlockSpec((TAP_ROWS, WIDE), lambda a: (a, 0)),
+            pl.BlockSpec((16, WIDE), lambda a: (TAPS * TAP_ROWS // 16, 0)),
+        ],
+        out_specs=[
+            pl.BlockSpec((1, TAPS, COUT, CIN), lambda a: (a, 0, 0, 0)),
+            pl.BlockSpec((1, COUT), lambda a: (0, 0)),
+        ],
+        compiler_params=pltpu.CompilerParams(vmem_limit_bytes=12 * 1024 * 1024),
+    )(summed, summed)
+    bias_grad = bias_grad.reshape(COUT)
     out_grad = jnp.transpose(grad, (2, 1, 0))[None]
     owned_score = owned[:CAP, :LON_DEV].reshape(1, 1, CAP * LON_DEV)
     return (out_grad, owned_score, weight_grad, bias_grad)

time: 91.2 us -> 83.3 us (0.913)
  other arithmetic: 6.15 us -> 0 us
  Pallas kernels: 81.7 us -> 78.8 us
  local copies, waits for them, and re-layouts: 2.58 us -> 3.73 us
    mul x2 -> x0, other arithmetic: 6.15 us -> none  [the longest x1 5.35 us: body(): summed[:25, :COUT, :CIN].astype(jnp.float32) * factor]
    pallas_call x1 -> x2, Pallas kernels: 81.7 us -> 78.8 us  [the longest x1 75.2 us: body(): pl.pallas_call(whole_kernel, out_shape=[jax.ShapeDtypeStruct((ROWS, WIDE)...]
    unnamed x4 -> x5, local copies, waits for them, and re-layouts: 1.27 us -> 2.42 us
where the time goes in v4:
time: 83.3 us; the launch traced here: 83.1 us
  Pallas kernels  78.8 us (95%)
  local copies, waits for them, and re-layouts  3.73 us (4%)
    pallas_call x1, Pallas kernels, body(): pl.pallas_call(whole_kernel, out_shape=[jax.ShapeDtypeStruct((ROWS, WIDE)...  75.2 us
    pallas_call x1, Pallas kernels, body(): pl.pallas_call(finish_kernel, grid=(TAPS,), out_shape=[jax.ShapeDtypeStru...  3.57 us
    unnamed x5, local copies, waits for them, and re-layouts  2.42 us

profile of v4, /device:TPU:1, one launch (start us, length us, event | category | flops | bytes accessed | tf_op | source)
XLA Modules:
  0.0 83.1 jit_solution(9915303718870200389)
XLA Ops:
  0.6 75.2 %shard_map.111 = (bf16[2048,640]{1,0:T(8,128)(2,1)}, bf16[45,16,73]{2,1,0:T(8,128)(2,1)}, f32[8,128]{1,0:T(8,128)}) custom-call(bf16[20,45,641]{2,1,0:T(8,128)(2,1)} %bitcast.14, bf16[5,5,73,641]{3,2,1,0:T(8,128)(2,1)} %w_hbm.1, f32[45,16,73]{2,1,0:T(8,128)} %bitcast.15, bf16[5,64,768]{2,1,0:T(8,128)(2,1)} %constant.4.clone.places_hbm, ...), custom_call_target="tpu_custom_call" | custom-call | flops 6442450944 | bytes 16777216 | tf_op jit(solution)/shard_map/pallas_call | solution.py:618
  75.8 1.3 %reshape.22 = f32[1,1,270]{2,1,0:T(1,128)} reshape(f32[6,45]{1,0:T(8,128)} %bitcast.13) | data formatting | bytes 2160 | tf_op jit(solution)/shard_map/reshape | solution.py:656
  77.1 0.0 copy-start
  77.1 1.7 %copy-done = bf16[2048,640]{1,0:T(8,128)(2,1)S(1)} copy-done((bf16[2048,640]{1,0:T(8,128)(2,1)S(1)}, bf16[2048,640]{1,0:T(8,128)(2,1)}, u32[]{:S(2)}) %copy-start) | copy-done | bytes 2621464
  78.9 0.0 copy-start.1
  78.9 3.6 %shard_map.112 = (f32[5,5,73,641]{3,2,1,0:T(8,128)}, f32[1,73]{1,0:T(1,128)}) custom-call(bf16[2048,640]{1,0:T(8,128)(2,1)S(1)} %copy-done, bf16[2048,640]{1,0:T(8,128)(2,1)S(1)} %copy-done), custom_call_target="tpu_custom_call" | custom-call | tf_op jit(solution)/shard_map/pallas_call | solution.py:637
  82.5 0.0 copy-done.1
  82.5 0.7 copy.13
Async XLA Ops:
  77.1 1.7 %copy-start = (bf16[2048,640]{1,0:T(8,128)(2,1)S(1)}, bf16[2048,640]{1,0:T(8,128)(2,1)}, u32[]{:S(2)}) copy-start(bf16[2048,640]{1,0:T(8,128)(2,1)} %get-tuple-element.11.main.extra) | copy-start | bytes 7864324
  78.9 3.6 %copy-start.1 = (bf16[45,16,73]{2,1,0:T(8,128)(2,1)S(1)}, bf16[45,16,73]{2,1,0:T(8,128)(2,1)}, u32[]{:S(2)}) copy-start(bf16[45,16,73]{2,1,0:T(8,128)(2,1)} %get-tuple-element.9) | copy-start | bytes 315364

commit v5 on v4

--- a/solution.py
+++ b/solution.py
@@ -150,7 +150,17 @@
         send(block, block, send_sems.at[k, 4 + s], recv_sems.at[k, 4 + s], moved(at, axis, delta))
 
 
-def all_reduce(at, out, core_rx, cur, rxs, shared, send_sems, recv_sems):
+def spread(at, out, k, dy, dx, send_sem, recv_sem, there):
+    first, second = ORDERS[k][0], ORDERS[k][1]
+    row = lax.rem(at[first] + 4 - dx, 4) * SIZES[k][0] + lax.rem(at[second] + 4 - dy, 4) * SIZES[k][1]
+    block = place(at, out, k, row, SIZES[k][1])
+    if there is None:
+        finish(block, send_sem, recv_sem, at).wait_recv()
+    else:
+        send(block, block, send_sem, recv_sem, there)
+
+
+def all_reduce(at, out, core_rx, cur, rxs, shared, send_sems, recv_sems, mid_recv, far_recv):
     row = [0] * PARTS
     partner = moved(at, "core", 1)
     for s in range(3):
@@ -195,18 +205,37 @@
                 gather(at, out, k, 2, row[k], send_sems, recv_sems)
             else:
                 launch(at, k, s + 1, cur, rxs, send_sems, recv_sems)
-    for s in (2, 1, 0):
-        for k in (2, 0, 1):
-            if k == 2 and s == 2:
-                continue
-            axis, rows = ORDERS[k][s], SIZES[k][s]
-            finish(rxs[k][s], send_sems.at[k, 4 + s], recv_sems.at[k, 4 + s], at).wait_recv()
-            row[k] = row[k] - at[axis] * rows
-            if s > 0:
-                gather(at, out, k, s - 1, row[k], send_sems, recv_sems)
-            else:
-                block = place(at, out, k, 0, PART_ROWS[k])
-                send(block, block, send_sems.at[k, 7], recv_sems.at[k, 7], partner)
+    def arrived(k, s):
+        finish(rxs[k][s], send_sems.at[k, 4 + s], recv_sems.at[k, 4 + s], at).wait_recv()
+
+    def onward(k, dy):
+        first = ORDERS[k][0]
+        for dx in (2, 1, 3):
+            spread(at, out, k, dy, 0, send_sems.at[k, 4], far_recv.at[k, 4 * dx + dy], moved(at, first, dx))
+        spread(at, out, k, dy, 0, send_sems.at[k, 7], recv_sems.at[k, 7], partner)
+
+    for k in range(2):
+        arrived(k, 2)
+        for dy in (2, 1, 3):
+            there = moved(at, ORDERS[k][1], dy)
+            spread(at, out, k, 0, 0, send_sems.at[k, 5], mid_recv.at[k, dy], there)
+        onward(k, 0)
+    arrived(2, 1)
+    row[2] = row[2] - at["x"] * SIZES[2][1]
+    gather(at, out, 2, 0, row[2], send_sems, recv_sems)
+    for dy in (1, 3, 2):
+        for k in range(2):
+            spread(at, out, k, dy, 0, send_sems.at[k, 5], mid_recv.at[k, dy], None)
+            onward(k, dy)
+    for dy in (0, 1, 3, 2):
+        if dy == 2:
+            arrived(2, 0)
+            block = place(at, out, 2, 0, PART_ROWS[2])
+            send(block, block, send_sems.at[2, 7], recv_sems.at[2, 7], partner)
+        for dx in (1, 3, 2):
+            for k in range(2):
+                spread(at, out, k, dy, dx, send_sems.at[k, 4], far_recv.at[k, 4 * dx + dy], None)
+                spread(at, out, k, dy, dx, send_sems.at[k, 7], recv_sems.at[k, 7], partner)
     for k in (2, 0, 1):
         finish(core_rx[k], send_sems.at[k, 7], recv_sems.at[k, 7], partner).wait_recv()
     for k in range(PARTS):
@@ -230,6 +259,7 @@
             shapes.append(pltpu.VMEM((EXTENT[axis] - 1, size, LANES), jnp.bfloat16))
     shapes.append(pltpu.VMEM((4, 32, LANES), jnp.bfloat16))
     shapes += [pltpu.SemaphoreType.DMA((PARTS, 8)), pltpu.SemaphoreType.DMA((PARTS, 8))]
+    shapes += [pltpu.SemaphoreType.DMA((2, 4)), pltpu.SemaphoreType.DMA((2, 16))]
     return shapes
 
 
@@ -418,7 +448,7 @@
     return total + jnp.dot(edge_stacked[...], margin[a, :, lanes], preferred_element_type=jnp.float32)
 
 
-def shared_terms(x, margin, stacked, edge_stacked, fifth, fifth_sent, tails, extra):
+def shared_terms(x, margin, stacked, edge_stacked, fifth, fifth_sent, tails):
     def one(a, _):
         total = product(a, slice(512, 768), x, margin, stacked, edge_stacked)
         rows = pl.ds(pl.multiple_of(a * TAP_ROWS, 16), TAP_ROWS)
@@ -427,17 +457,19 @@
         tails[a, :, 0:TAP_ROWS] = jnp.transpose(total[:, LANES:])[0:8, :]
         return 0
 
+    tails[...] = jnp.zeros((TAPS, 8, 512), jnp.float32)
     lax.fori_loop(0, TAPS, one, 0)
     spare = ROWS - TAPS * TAP_ROWS
     fifth[TAPS * TAP_ROWS : ROWS, :] = jnp.zeros((spare, LANES), jnp.float32)
-    fifth_sent[TAPS * TAP_ROWS : ROWS, :] = jnp.zeros((spare, LANES), jnp.bfloat16)
-    extra[...] = jnp.zeros((16, 512), jnp.float32)
-    for a in range(TAPS):
-        extra[a : a + 1, 0:TAP_ROWS] = tails[a, 0:1, 0:TAP_ROWS]
-    extra[TAPS : TAPS + 1, 0:TAP_ROWS] = tails[2, 1:2, 0:TAP_ROWS]
-
-
-def weight_terms(half, x, margin, stacked, edge_stacked, extra, into):
+    for n in range(TAPS + 1):
+        a, channel = (n, 0) if n < TAPS else (2, 1)
+        for q in range(4):
+            row = TAPS * TAP_ROWS + 4 * n + q
+            fifth[row : row + 1, :] = tails[a, channel : channel + 1, q * LANES : (q + 1) * LANES]
+    fifth_sent[TAPS * TAP_ROWS : ROWS, :] = fifth[TAPS * TAP_ROWS : ROWS, :].astype(jnp.bfloat16)
+
+
+def weight_terms(half, x, margin, stacked, edge_stacked, into):
     lanes = pl.ds(pl.multiple_of(half * 256, 256), 256)
 
     def one(a, _):
@@ -449,10 +481,8 @@
 
     lax.fori_loop(0, TAPS, one, 0)
     first = TAPS * TAP_ROWS
-    more = extra[:, lanes].astype(into.dtype)
     for k in range(2):
-        into[k, first : first + 16, :] = more[:, k * LANES : (k + 1) * LANES]
-        into[k, first + 16 : ROWS, :] = jnp.zeros((ROWS - first - 16, LANES), into.dtype)
+        into[k, first:ROWS, :] = jnp.zeros((ROWS - first, LANES), into.dtype)
 
 
 def own_scores(starts, score_rx, owned):
@@ -467,7 +497,7 @@
         low = jnp.where(lane < LON_DEV, pair, 0.0)
         high = jnp.where(lane < LON_DEV, pltpu.roll(pair, LANES - PITCH, 1), 0.0)
         total = total + jnp.where(wanted == 2 * q, low, 0.0) + jnp.where(wanted == 2 * q + 1, high, 0.0)
-    owned[...] = total
+    owned[...] = jnp.concatenate([total[s : s + 1, 0:LON_DEV] for s in range(CAP)], axis=1)
 
 
 def whole_kernel(
@@ -477,12 +507,12 @@
     scratch = scratch[12:]
     (
         staged, edges, halo, margin, taps, edge_taps, to_score, values, gradients, gathered, score, score_rx,
-        stacked, edge_stacked, theirs, mine, fifth, fifth_sent, tails, extra, near_send, near_recv,
-    ) = scratch[:22]
-    core_rx, rest = scratch[22:25], scratch[25:]
+        stacked, edge_stacked, theirs, mine, fifth, fifth_sent, tails, near_send, near_recv,
+    ) = scratch[:21]
+    core_rx, rest = scratch[21:24], scratch[24:]
     cur = [rest[3 * k : 3 * k + 3] for k in range(PARTS)]
     rxs = [rest[8 + 3 * k : 11 + 3 * k] for k in range(PARTS)]
-    shared, send_sems, recv_sems = rest[16:19]
+    shared, send_sems, recv_sems, mid_recv, far_recv = rest[16:21]
     at = position()
     member, lon = lax.axis_index("member"), lax.axis_index("lon")
     ahead = (member, lax.rem(lon + 1, GROUPS))
@@ -505,11 +535,11 @@
     edge = jnp.dot(picks[...], x[...], preferred_element_type=jnp.float32).astype(jnp.bfloat16)
     edges[0] = edge[:PITCH]
     edges[1] = edge[PITCH:]
+    loads[2].wait()
+    stage_weight(w, staged)
     pl.semaphore_wait(barrier, count)
     send_to(edges.at[0], halo.at[0], near_send.at[0], near_recv.at[0], ahead)
     send_to(edges.at[1], halo.at[1], near_send.at[1], near_recv.at[1], behind)
-    loads[2].wait()
-    stage_weight(w, staged)
     forward_own(x, staged, taps)
     loads[3].wait()
     loads[4].wait()
@@ -536,22 +566,20 @@
     finish(gathered.at[0:7], near_send.at[3], near_recv.at[3], at).wait_recv()
     stack_gradient(gathered, packed, stacked, edge_stacked, places)
     core, partner = at["core"], moved(at, "core", 1)
-    shared_terms(x, margin, stacked, edge_stacked, fifth, fifth_sent, tails, extra)
+    weight_terms(1 - core, x, margin, stacked, edge_stacked, theirs)
+    for k in range(2):
+        send(theirs.at[k], core_rx[k], send_sems.at[k, 0], recv_sems.at[k, 0], partner)
+    shared_terms(x, margin, stacked, edge_stacked, fifth, fifth_sent, tails)
     source = fifth_sent.at[pl.ds(pl.multiple_of((1 - core) * 1024, 16), 1024)]
     send(source, core_rx[2], send_sems.at[2, 0], recv_sems.at[2, 0], partner)
-    weight_terms(1 - core, x, margin, stacked, edge_stacked, extra, theirs)
-    for k in range(2):
-        send(theirs.at[k], core_rx[k], send_sems.at[k, 0], recv_sems.at[k, 0], partner)
-    add_core(at, 2, fifth, core_rx, cur, send_sems, recv_sems)
-    launch(at, 2, 0, cur, rxs, send_sems, recv_sems)
-    weight_terms(core, x, margin, stacked, edge_stacked, extra, mine)
-    for k in range(2):
-        add_core(at, k, mine, core_rx, cur, send_sems, recv_sems)
+    weight_terms(core, x, margin, stacked, edge_stacked, mine)
+    for k, own in ((0, mine), (1, mine), (2, fifth)):
+        add_core(at, k, own, core_rx, cur, send_sems, recv_sems)
         launch(at, k, 0, cur, rxs, send_sems, recv_sems)
     write_gradient(packed, grad_out)
     finish(score_rx.at[0:7], near_send.at[4], near_recv.at[4], at).wait_recv()
     own_scores(starts, score_rx, owned)
-    all_reduce(at, out, core_rx, cur, rxs, shared, send_sems, recv_sems)
+    all_reduce(at, out, core_rx, cur, rxs, shared, send_sems, recv_sems, mid_recv, far_recv)
     finish(values.at[0:7], near_send.at[2], near_recv.at[2], at).wait_send()
     finish(gathered.at[0:7], near_send.at[3], near_recv.at[3], at).wait_send()
     finish(score_rx.at[0:7], near_send.at[4], near_recv.at[4], at).wait_send()
@@ -591,25 +619,27 @@
         pltpu.VMEM((ROWS, LANES), jnp.float32),
         pltpu.VMEM((ROWS, LANES), jnp.bfloat16),
         pltpu.VMEM((TAPS, 8, 512), jnp.float32),
-        pltpu.VMEM((16, 512), jnp.float32),
         pltpu.SemaphoreType.DMA((5,)),
         pltpu.SemaphoreType.DMA((5,)),
     ] + reduce_scratch()
 
 
-def finish_kernel(main, extra, weight_grad, bias_grad):
+def finish_kernel(main, low, high, weight_grad, bias_grad):
     factor = 1.0 / math.sqrt(MEMBERS * LAT * LON_DEV * GROUPS)
     a = pl.program_id(0)
-    more = extra[...].astype(jnp.float32) * factor
-    number = lax.broadcasted_iota(jnp.int32, (16, WIDE), 0)
-    last = jnp.sum(jnp.where(number == a, more, 0.0), axis=0, keepdims=True)
-    last = jnp.transpose(jnp.broadcast_to(last[:, 0:512], (8, 512)))
+    more = jnp.concatenate([low[...].astype(jnp.float32), high[...].astype(jnp.float32)], axis=0) * factor
+    number = lax.broadcasted_iota(jnp.int32, (32, LANES), 0)
+    pieces = [
+        jnp.sum(jnp.where(number == 4 * a + q, more, 0.0), axis=0, keepdims=True) for q in range(4)
+    ]
+    last = jnp.transpose(jnp.broadcast_to(jnp.concatenate(pieces, axis=1), (8, 512)))
     for b in range(TAPS):
         weight_grad[0, b, :, 0:WIDE] = (
             main[b * CHAN : (b + 1) * CHAN, :].astype(jnp.float32)[:COUT, :] * factor
         )
         weight_grad[0, b, :, WIDE:CIN] = last[b * CHAN : b * CHAN + COUT, 0:1]
-    bias_grad[...] = more[TAPS : TAPS + 1, 2 * CHAN : 2 * CHAN + COUT]
+    bias = jnp.concatenate([more[4 * TAPS + q : 4 * TAPS + q + 1, :] for q in range(4)], axis=1)
+    bias_grad[...] = bias[:, 2 * CHAN : 2 * CHAN + COUT]
 
 
 def body(fields, weight, out_bias, observed, widths, owner_start):
@@ -620,7 +650,7 @@
         out_shape=[
             jax.ShapeDtypeStruct((ROWS, WIDE), jnp.bfloat16),
             jax.ShapeDtypeStruct((LON_DEV, LAT, COUT), jnp.bfloat16),
-            jax.ShapeDtypeStruct((8, LANES), jnp.float32),
+            jax.ShapeDtypeStruct((1, CAP * LON_DEV), jnp.float32),
         ],
         in_specs=[hbm] * 5 + [vmem] * 2 + [pl.BlockSpec(memory_space=pltpu.SMEM)],
         out_specs=[vmem] * 3,
@@ -643,17 +673,18 @@
         ],
         in_specs=[
             pl.BlockSpec((TAP_ROWS, WIDE), lambda a: (a, 0)),
-            pl.BlockSpec((16, WIDE), lambda a: (TAPS * TAP_ROWS // 16, 0)),
+            pl.BlockSpec((16, LANES), lambda a: (TAPS * TAP_ROWS // 16, 4)),
+            pl.BlockSpec((16, LANES), lambda a: (TAPS * TAP_ROWS // 16 + 1, 4)),
         ],
         out_specs=[
             pl.BlockSpec((1, TAPS, COUT, CIN), lambda a: (a, 0, 0, 0)),
             pl.BlockSpec((1, COUT), lambda a: (0, 0)),
         ],
-        compiler_params=pltpu.CompilerParams(vmem_limit_bytes=12 * 1024 * 1024),
-    )(summed, summed)
+        compiler_params=pltpu.CompilerParams(vmem_limit_bytes=58 * 1024 * 1024),
+    )(summed, summed, summed)
     bias_grad = bias_grad.reshape(COUT)
     out_grad = jnp.transpose(grad, (2, 1, 0))[None]
-    owned_score = owned[:CAP, :LON_DEV].reshape(1, 1, CAP * LON_DEV)
+    owned_score = owned.reshape(1, 1, CAP * LON_DEV)
     return (out_grad, owned_score, weight_grad, bias_grad)
 
 

time: 83.3 us -> 80.5 us (0.966)
  local copies, waits for them, and re-layouts: 3.73 us -> 1.24 us
    pallas_call x1, Pallas kernels: 75.2 us -> 72.8 us  [body(): pl.pallas_call(whole_kernel, out_shape=[jax.ShapeDtypeStruct((ROWS, WIDE)...]
    pallas_call x1, Pallas kernels: 3.57 us -> 5.6 us  [body(): pl.pallas_call(finish_kernel, grid=(TAPS,), out_shape=[jax.ShapeDtypeStru...]
    reshape x1 -> x0, local copies, waits for them, and re-layouts: 1.32 us -> none  [body(): owned_score = owned[:CAP, :LON_DEV].reshape(1, 1, CAP * LON_DEV)]
    unnamed x5 -> x6, local copies, waits for them, and re-layouts: 2.42 us -> 1.24 us
where the time goes in v5:
time: 80.5 us; the launch traced here: 80.3 us
  Pallas kernels  78.4 us (97%)
  local copies, waits for them, and re-layouts  1.24 us (2%)
    pallas_call x1, Pallas kernels, body(): pl.pallas_call(whole_kernel, out_shape=[jax.ShapeDtypeStruct((ROWS, WIDE)...  72.8 us
    pallas_call x1, Pallas kernels, body(): pl.pallas_call(finish_kernel, grid=(TAPS,), out_shape=[jax.ShapeDtypeStru...  5.6 us

profile of v5, /device:TPU:1, one launch (start us, length us, event | category | flops | bytes accessed | tf_op | source)
XLA Modules:
  0.0 80.3 jit_solution(9478859632034435891)
XLA Ops:
  0.6 72.8 %shard_map.111 = (bf16[2048,640]{1,0:T(8,128)(2,1)}, bf16[45,16,73]{2,1,0:T(8,128)(2,1)}, f32[1,270]{1,0:T(1,128)}) custom-call(bf16[20,45,641]{2,1,0:T(8,128)(2,1)} %bitcast.14, bf16[5,5,73,641]{3,2,1,0:T(8,128)(2,1)} %w_hbm.1, f32[45,16,73]{2,1,0:T(8,128)} %bitcast.15, bf16[5,64,768]{2,1,0:T(8,128)(2,1)} %constant.4.clone.places_hbm, ...), custom_call_target="tpu_custom_call" | custom-call | flops 6442450944 | bytes 16777216 | tf_op jit(solution)/shard_map/pallas_call | solution.py:648
  73.4 0.0 copy-start
  73.4 0.0 copy-start.1
  73.5 5.6 %shard_map.112 = (f32[5,5,73,641]{3,2,1,0:T(8,128)}, f32[1,73]{1,0:T(1,128)}) custom-call(bf16[2048,640]{1,0:T(8,128)(2,1)} %get-tuple-element.11.main.low.high, bf16[2048,640]{1,0:T(8,128)(2,1)} %get-tuple-element.11.main.low.high, bf16[2048,640]{1,0:T(8,128)(2,1)} %get-tuple-element.11.main.low.high), custom_call_target="tpu_custom_call" | custom-call | tf_op jit(solution)/shard_map/pallas_call | solution.py:667
  79.1 0.0 copy-done
  79.1 0.7 copy.14
  79.7 0.0 copy-done.1
  79.7 0.6 copy.15
Async XLA Ops:
  73.4 5.6 %copy-start = (bf16[45,16,73]{2,1,0:T(8,128)(2,1)S(1)}, bf16[45,16,73]{2,1,0:T(8,128)(2,1)}, u32[]{:S(2)}) copy-start(bf16[45,16,73]{2,1,0:T(8,128)(2,1)} %get-tuple-element.9) | copy-start | bytes 315364
  73.4 6.3 %copy-start.1 = (f32[1,270]{1,0:T(1,128)S(1)}, f32[1,270]{1,0:T(1,128)}, u32[]{:S(2)}) copy-start(f32[1,270]{1,0:T(1,128)} %get-tuple-element.10) | copy-start | bytes 3244

commit v6 on v5

--- a/solution.py
+++ b/solution.py
@@ -114,9 +114,8 @@
 
 def place(at, out, k, row, rows):
     if k == 2:
-        return out.at[pl.ds(pl.multiple_of(at["core"] * 1024 + row, 16), rows), 512:640]
-    lane = pl.multiple_of((2 * at["core"] + k) * LANES, LANES)
-    return out.at[pl.ds(pl.multiple_of(row, 16), rows), pl.ds(lane, LANES)]
+        return out.at[4, pl.ds(pl.multiple_of(at["core"] * 1024 + row, 16), rows), :]
+    return out.at[2 * at["core"] + k, pl.ds(pl.multiple_of(row, 16), rows), :]
 
 
 def launch(at, k, s, cur, rxs, send_sems, recv_sems):
@@ -624,22 +623,41 @@
     ] + reduce_scratch()
 
 
-def finish_kernel(main, low, high, weight_grad, bias_grad):
+def finish_kernel(
+    summed, grad_in, owned_in, weight_grad, grad_out, owned_out, bias_grad, main, wide, in_sems, out_sems, pass_sems
+):
     factor = 1.0 / math.sqrt(MEMBERS * LAT * LON_DEV * GROUPS)
-    a = pl.program_id(0)
-    more = jnp.concatenate([low[...].astype(jnp.float32), high[...].astype(jnp.float32)], axis=0) * factor
-    number = lax.broadcasted_iota(jnp.int32, (32, LANES), 0)
-    pieces = [
-        jnp.sum(jnp.where(number == 4 * a + q, more, 0.0), axis=0, keepdims=True) for q in range(4)
+    passed = [
+        pltpu.make_async_copy(grad_in, grad_out, pass_sems.at[0]),
+        pltpu.make_async_copy(owned_in, owned_out, pass_sems.at[1]),
     ]
-    last = jnp.transpose(jnp.broadcast_to(jnp.concatenate(pieces, axis=1), (8, 512)))
-    for b in range(TAPS):
-        weight_grad[0, b, :, 0:WIDE] = (
-            main[b * CHAN : (b + 1) * CHAN, :].astype(jnp.float32)[:COUT, :] * factor
-        )
-        weight_grad[0, b, :, WIDE:CIN] = last[b * CHAN : b * CHAN + COUT, 0:1]
+    first = TAPS * TAP_ROWS
+    tail = (TAPS - 1, slice(first, ROWS))
+    loads = [pltpu.make_async_copy(summed.at[tail], main.at[tail], in_sems.at[TAPS])]
+    for a in range(TAPS):
+        rows = (slice(None), slice(a * TAP_ROWS, (a + 1) * TAP_ROWS))
+        loads.append(pltpu.make_async_copy(summed.at[rows], main.at[rows], in_sems.at[a]))
+    for copy in loads + passed:
+        copy.start()
+    loads[0].wait()
+    more = main[TAPS - 1, first:ROWS, :].astype(jnp.float32) * factor
     bias = jnp.concatenate([more[4 * TAPS + q : 4 * TAPS + q + 1, :] for q in range(4)], axis=1)
     bias_grad[...] = bias[:, 2 * CHAN : 2 * CHAN + COUT]
+    stores = []
+    for a in range(TAPS):
+        last = jnp.concatenate([more[4 * a + q : 4 * a + q + 1, :] for q in range(4)], axis=1)
+        last = jnp.transpose(jnp.broadcast_to(last, (8, 512)))
+        loads[a + 1].wait()
+        for b in range(TAPS):
+            base, n = a * TAP_ROWS + b * CHAN, a * TAPS + b
+            for block in range(TAPS):
+                part = main[block, base : base + CHAN, :].astype(jnp.float32) * factor
+                wide[n, :, block * LANES : (block + 1) * LANES] = part[:COUT]
+            wide[n, :, WIDE:CIN] = last[b * CHAN : b * CHAN + COUT, 0:1]
+            stores.append(pltpu.make_async_copy(wide.at[n], weight_grad.at[n], out_sems.at[n]))
+            stores[-1].start()
+    for copy in stores + passed:
+        copy.wait()
 
 
 def body(fields, weight, out_bias, observed, widths, owner_start):
@@ -648,7 +666,7 @@
     summed, grad, owned = pl.pallas_call(
         whole_kernel,
         out_shape=[
-            jax.ShapeDtypeStruct((ROWS, WIDE), jnp.bfloat16),
+            jax.ShapeDtypeStruct((TAPS, ROWS, LANES), jnp.bfloat16),
             jax.ShapeDtypeStruct((LON_DEV, LAT, COUT), jnp.bfloat16),
             jax.ShapeDtypeStruct((1, CAP * LON_DEV), jnp.float32),
         ],
@@ -664,24 +682,26 @@
         jnp.asarray(margin_places(), jnp.bfloat16), jnp.asarray(edge_picks(), jnp.bfloat16),
         out_bias.reshape(1, COUT), widths.reshape(1, COUT), owner_start[0],
     )
-    weight_grad, bias_grad = pl.pallas_call(
+    weight_grad, grad, owned, bias_grad = pl.pallas_call(
         finish_kernel,
-        grid=(TAPS,),
         out_shape=[
-            jax.ShapeDtypeStruct((TAPS, TAPS, COUT, CIN), jnp.float32),
+            jax.ShapeDtypeStruct((TAPS * TAPS, COUT, CIN), jnp.float32),
+            jax.ShapeDtypeStruct((LON_DEV, LAT, COUT), jnp.bfloat16),
+            jax.ShapeDtypeStruct((1, CAP * LON_DEV), jnp.float32),
             jax.ShapeDtypeStruct((1, COUT), jnp.float32),
         ],
-        in_specs=[
-            pl.BlockSpec((TAP_ROWS, WIDE), lambda a: (a, 0)),
-            pl.BlockSpec((16, LANES), lambda a: (TAPS * TAP_ROWS // 16, 4)),
-            pl.BlockSpec((16, LANES), lambda a: (TAPS * TAP_ROWS // 16 + 1, 4)),
-        ],
-        out_specs=[
-            pl.BlockSpec((1, TAPS, COUT, CIN), lambda a: (a, 0, 0, 0)),
-            pl.BlockSpec((1, COUT), lambda a: (0, 0)),
+        in_specs=[hbm] * 3,
+        out_specs=[hbm] * 3 + [vmem],
+        scratch_shapes=[
+            pltpu.VMEM((TAPS, ROWS, LANES), jnp.bfloat16),
+            pltpu.VMEM((TAPS * TAPS, COUT, CIN), jnp.float32),
+            pltpu.SemaphoreType.DMA((TAPS + 1,)),
+            pltpu.SemaphoreType.DMA((TAPS * TAPS,)),
+            pltpu.SemaphoreType.DMA((2,)),
         ],
         compiler_params=pltpu.CompilerParams(vmem_limit_bytes=58 * 1024 * 1024),
-    )(summed, summed, summed)
+    )(summed, grad, owned)
+    weight_grad = weight_grad.reshape(TAPS, TAPS, COUT, CIN)
     bias_grad = bias_grad.reshape(COUT)
     out_grad = jnp.transpose(grad, (2, 1, 0))[None]
     owned_score = owned.reshape(1, 1, CAP * LON_DEV)

time: 80.5 us -> 81.2 us (level)
  Pallas kernels: 78.4 us -> 80.4 us
  local copies, waits for them, and re-layouts: 1.24 us -> 0 us
    pallas_call x2, Pallas kernels: 78.4 us -> 80.4 us  [the longest x1 72.8 us: body(): pl.pallas_call(whole_kernel, out_shape=[jax.ShapeDtypeStruct((TAPS, ROWS,...]
    unnamed x6 -> x0, local copies, waits for them, and re-layouts: 1.24 us -> none
where the time goes in v6:
time: 81.2 us; the launch traced here: 81 us
  Pallas kernels  80.4 us (99%)
    pallas_call x1, Pallas kernels, body(): pl.pallas_call(whole_kernel, out_shape=[jax.ShapeDtypeStruct((TAPS, ROWS,...  72.8 us
    pallas_call x1, Pallas kernels, body(): pl.pallas_call(finish_kernel, out_shape=[jax.ShapeDtypeStruct((TAPS * TAP...  7.55 us

profile of v6, /device:TPU:1, one launch (start us, length us, event | category | flops | bytes accessed | tf_op | source)
XLA Modules:
  0.0 81.0 jit_solution(13395663523739640057)
XLA Ops:
  0.6 72.8 %shard_map.111 = (bf16[5,2048,128]{2,1,0:T(8,128)(2,1)}, bf16[45,16,73]{2,1,0:T(8,128)(2,1)}, f32[1,270]{1,0:T(1,128)}) custom-call(bf16[20,45,641]{2,1,0:T(8,128)(2,1)} %bitcast.14, bf16[5,5,73,641]{3,2,1,0:T(8,128)(2,1)} %w_hbm.1, f32[45,16,73]{2,1,0:T(8,128)} %bitcast.15, bf16[5,64,768]{2,1,0:T(8,128)(2,1)} %constant.4.clone.places_hbm, ...), custom_call_target="tpu_custom_call" | custom-call | flops 6442450944 | bytes 16777216 | tf_op jit(solution)/shard_map/pallas_call | solution.py:666
  73.4 7.5 %shard_map.112 = (f32[25,73,641]{2,1,0:T(8,128)}, bf16[45,16,73]{2,1,0:T(8,128)(2,1)}, f32[1,270]{1,0:T(1,128)}, f32[1,73]{1,0:T(1,128)}) custom-call(bf16[5,2048,128]{2,1,0:T(8,128)(2,1)} %get-tuple-element.11.summed, bf16[45,16,73]{2,1,0:T(8,128)(2,1)} %get-tuple-element.12.grad_in, f32[1,270]{1,0:T(1,128)} %get-tuple-element.13.owned_in), custom_call_target="tpu_custom_call" | custom-call | tf_op jit(solution)/shard_map/pallas_call | solution.py:685

commit v7 on v5

--- a/solution.py
+++ b/solution.py
@@ -164,7 +164,7 @@
     row = [0] * PARTS
     partner = moved(at, "core", 1)
     for s in range(3):
-        for k in (2, 0, 1):
+        for k in (2, 0, 1) if s == 2 else (0, 1, 2):
             if k == 2 and s == 2:
                 finish(shared.at[0:3], send_sems.at[k, 3], recv_sems.at[k, 3], at).wait_recv()
                 total = shared[0].astype(jnp.float32)
@@ -214,15 +214,15 @@
             spread(at, out, k, dy, 0, send_sems.at[k, 4], far_recv.at[k, 4 * dx + dy], moved(at, first, dx))
         spread(at, out, k, dy, 0, send_sems.at[k, 7], recv_sems.at[k, 7], partner)
 
+    arrived(2, 1)
+    row[2] = row[2] - at["x"] * SIZES[2][1]
+    gather(at, out, 2, 0, row[2], send_sems, recv_sems)
     for k in range(2):
         arrived(k, 2)
         for dy in (2, 1, 3):
             there = moved(at, ORDERS[k][1], dy)
             spread(at, out, k, 0, 0, send_sems.at[k, 5], mid_recv.at[k, dy], there)
         onward(k, 0)
-    arrived(2, 1)
-    row[2] = row[2] - at["x"] * SIZES[2][1]
-    gather(at, out, 2, 0, row[2], send_sems, recv_sems)
     for dy in (1, 3, 2):
         for k in range(2):
             spread(at, out, k, dy, 0, send_sems.at[k, 5], mid_recv.at[k, dy], None)
@@ -624,7 +624,17 @@
     ] + reduce_scratch()
 
 
-def finish_kernel(main, low, high, weight_grad, bias_grad):
+def finish_kernel(main, low, high, grad_in, owned_in, weight_grad, bias_grad, grad_out, owned_out, sems):
+    passed = [
+        pltpu.make_async_copy(grad_in, grad_out, sems.at[0]),
+        pltpu.make_async_copy(owned_in, owned_out, sems.at[1]),
+    ]
+
+    @pl.when(pl.program_id(0) == 0)
+    def _():
+        for copy in passed:
+            copy.start()
+
     factor = 1.0 / math.sqrt(MEMBERS * LAT * LON_DEV * GROUPS)
     a = pl.program_id(0)
     more = jnp.concatenate([low[...].astype(jnp.float32), high[...].astype(jnp.float32)], axis=0) * factor
@@ -640,6 +650,11 @@
         weight_grad[0, b, :, WIDE:CIN] = last[b * CHAN : b * CHAN + COUT, 0:1]
     bias = jnp.concatenate([more[4 * TAPS + q : 4 * TAPS + q + 1, :] for q in range(4)], axis=1)
     bias_grad[...] = bias[:, 2 * CHAN : 2 * CHAN + COUT]
+
+    @pl.when(pl.program_id(0) == TAPS - 1)
+    def _():
+        for copy in passed:
+            copy.wait()
 
 
 def body(fields, weight, out_bias, observed, widths, owner_start):
@@ -664,24 +679,31 @@
         jnp.asarray(margin_places(), jnp.bfloat16), jnp.asarray(edge_picks(), jnp.bfloat16),
         out_bias.reshape(1, COUT), widths.reshape(1, COUT), owner_start[0],
     )
-    weight_grad, bias_grad = pl.pallas_call(
+    weight_grad, bias_grad, grad, owned = pl.pallas_call(
         finish_kernel,
         grid=(TAPS,),
         out_shape=[
             jax.ShapeDtypeStruct((TAPS, TAPS, COUT, CIN), jnp.float32),
             jax.ShapeDtypeStruct((1, COUT), jnp.float32),
+            jax.ShapeDtypeStruct((LON_DEV, LAT, COUT), jnp.bfloat16),
+            jax.ShapeDtypeStruct((1, CAP * LON_DEV), jnp.float32),
         ],
         in_specs=[
             pl.BlockSpec((TAP_ROWS, WIDE), lambda a: (a, 0)),
             pl.BlockSpec((16, LANES), lambda a: (TAPS * TAP_ROWS // 16, 4)),
             pl.BlockSpec((16, LANES), lambda a: (TAPS * TAP_ROWS // 16 + 1, 4)),
+            hbm,
+            hbm,
         ],
         out_specs=[
             pl.BlockSpec((1, TAPS, COUT, CIN), lambda a: (a, 0, 0, 0)),
             pl.BlockSpec((1, COUT), lambda a: (0, 0)),
+            hbm,
+            hbm,
         ],
+        scratch_shapes=[pltpu.SemaphoreType.DMA((2,))],
         compiler_params=pltpu.CompilerParams(vmem_limit_bytes=58 * 1024 * 1024),
-    )(summed, summed, summed)
+    )(summed, summed, summed, grad, owned)
     bias_grad = bias_grad.reshape(COUT)
     out_grad = jnp.transpose(grad, (2, 1, 0))[None]
     owned_score = owned.reshape(1, 1, CAP * LON_DEV)

time: 80.5 us -> 80.2 us (level)
  local copies, waits for them, and re-layouts: 1.24 us -> 0 us
  Pallas kernels: 78.4 us -> 79.4 us
    pallas_call x1, Pallas kernels: 5.6 us -> 8.84 us  [body(): pl.pallas_call(finish_kernel, grid=(TAPS,), out_shape=[jax.ShapeDtypeStru...]
    pallas_call x1, Pallas kernels: 72.8 us -> 70.6 us  [body(): pl.pallas_call(whole_kernel, out_shape=[jax.ShapeDtypeStruct((ROWS, WIDE)...]
    unnamed x6 -> x0, local copies, waits for them, and re-layouts: 1.24 us -> none
where the time goes in v7:
time: 80.2 us; the launch traced here: 80 us
  Pallas kernels  79.4 us (99%)
    pallas_call x1, Pallas kernels, body(): pl.pallas_call(whole_kernel, out_shape=[jax.ShapeDtypeStruct((ROWS, WIDE)...  70.6 us
    pallas_call x1, Pallas kernels, body(): pl.pallas_call(finish_kernel, grid=(TAPS,), out_shape=[jax.ShapeDtypeStru...  8.84 us

profile of v7, /device:TPU:1, one launch (start us, length us, event | category | flops | bytes accessed | tf_op | source)
XLA Modules:
  0.0 80.0 jit_solution(10178844115372142233)
XLA Ops:
  0.6 70.6 %shard_map.111 = (bf16[2048,640]{1,0:T(8,128)(2,1)}, bf16[45,16,73]{2,1,0:T(8,128)(2,1)}, f32[1,270]{1,0:T(1,128)}) custom-call(bf16[20,45,641]{2,1,0:T(8,128)(2,1)} %bitcast.12, bf16[5,5,73,641]{3,2,1,0:T(8,128)(2,1)} %w_hbm.1, f32[45,16,73]{2,1,0:T(8,128)} %bitcast.13, bf16[5,64,768]{2,1,0:T(8,128)(2,1)} %constant.4.clone.places_hbm, ...), custom_call_target="tpu_custom_call" | custom-call | flops 6442450944 | bytes 16777216 | tf_op jit(solution)/shard_map/pallas_call | solution.py:663
  71.2 8.8 %shard_map.112 = (f32[5,5,73,641]{3,2,1,0:T(8,128)}, f32[1,73]{1,0:T(1,128)}, bf16[45,16,73]{2,1,0:T(8,128)(2,1)}, f32[1,270]{1,0:T(1,128)}) custom-call(bf16[2048,640]{1,0:T(8,128)(2,1)} %get-tuple-element.11.main.low.high, bf16[2048,640]{1,0:T(8,128)(2,1)} %get-tuple-element.11.main.low.high, bf16[2048,640]{1,0:T(8,128)(2,1)} %get-tuple-element.11.main.low.high, ...), custom_call_target="tpu_custom_call" | custom-call | tf_op jit(solution)/shard_map/pallas_call | solution.py:682

commit v8 on v6

--- a/solution.py
+++ b/solution.py
@@ -163,7 +163,7 @@
     row = [0] * PARTS
     partner = moved(at, "core", 1)
     for s in range(3):
-        for k in (2, 0, 1):
+        for k in (2, 0, 1) if s == 2 else (0, 1, 2):
             if k == 2 and s == 2:
                 finish(shared.at[0:3], send_sems.at[k, 3], recv_sems.at[k, 3], at).wait_recv()
                 total = shared[0].astype(jnp.float32)
@@ -213,15 +213,15 @@
             spread(at, out, k, dy, 0, send_sems.at[k, 4], far_recv.at[k, 4 * dx + dy], moved(at, first, dx))
         spread(at, out, k, dy, 0, send_sems.at[k, 7], recv_sems.at[k, 7], partner)
 
+    arrived(2, 1)
+    row[2] = row[2] - at["x"] * SIZES[2][1]
+    gather(at, out, 2, 0, row[2], send_sems, recv_sems)
     for k in range(2):
         arrived(k, 2)
         for dy in (2, 1, 3):
             there = moved(at, ORDERS[k][1], dy)
             spread(at, out, k, 0, 0, send_sems.at[k, 5], mid_recv.at[k, dy], there)
         onward(k, 0)
-    arrived(2, 1)
-    row[2] = row[2] - at["x"] * SIZES[2][1]
-    gather(at, out, 2, 0, row[2], send_sems, recv_sems)
     for dy in (1, 3, 2):
         for k in range(2):
             spread(at, out, k, dy, 0, send_sems.at[k, 5], mid_recv.at[k, dy], None)
@@ -624,20 +624,16 @@
 
 
 def finish_kernel(
-    summed, grad_in, owned_in, weight_grad, grad_out, owned_out, bias_grad, main, wide, in_sems, out_sems, pass_sems
+    summed, weight_grad, bias_grad, main, wide, in_sems, out_sems
 ):
     factor = 1.0 / math.sqrt(MEMBERS * LAT * LON_DEV * GROUPS)
-    passed = [
-        pltpu.make_async_copy(grad_in, grad_out, pass_sems.at[0]),
-        pltpu.make_async_copy(owned_in, owned_out, pass_sems.at[1]),
-    ]
     first = TAPS * TAP_ROWS
     tail = (TAPS - 1, slice(first, ROWS))
     loads = [pltpu.make_async_copy(summed.at[tail], main.at[tail], in_sems.at[TAPS])]
     for a in range(TAPS):
         rows = (slice(None), slice(a * TAP_ROWS, (a + 1) * TAP_ROWS))
         loads.append(pltpu.make_async_copy(summed.at[rows], main.at[rows], in_sems.at[a]))
-    for copy in loads + passed:
+    for copy in loads:
         copy.start()
     loads[0].wait()
     more = main[TAPS - 1, first:ROWS, :].astype(jnp.float32) * factor
@@ -656,7 +652,7 @@
             wide[n, :, WIDE:CIN] = last[b * CHAN : b * CHAN + COUT, 0:1]
             stores.append(pltpu.make_async_copy(wide.at[n], weight_grad.at[n], out_sems.at[n]))
             stores[-1].start()
-    for copy in stores + passed:
+    for copy in stores:
         copy.wait()
 
 
@@ -682,25 +678,22 @@
         jnp.asarray(margin_places(), jnp.bfloat16), jnp.asarray(edge_picks(), jnp.bfloat16),
         out_bias.reshape(1, COUT), widths.reshape(1, COUT), owner_start[0],
     )
-    weight_grad, grad, owned, bias_grad = pl.pallas_call(
+    weight_grad, bias_grad = pl.pallas_call(
         finish_kernel,
         out_shape=[
             jax.ShapeDtypeStruct((TAPS * TAPS, COUT, CIN), jnp.float32),
-            jax.ShapeDtypeStruct((LON_DEV, LAT, COUT), jnp.bfloat16),
-            jax.ShapeDtypeStruct((1, CAP * LON_DEV), jnp.float32),
             jax.ShapeDtypeStruct((1, COUT), jnp.float32),
         ],
-        in_specs=[hbm] * 3,
-        out_specs=[hbm] * 3 + [vmem],
+        in_specs=[hbm],
+        out_specs=[hbm, vmem],
         scratch_shapes=[
             pltpu.VMEM((TAPS, ROWS, LANES), jnp.bfloat16),
             pltpu.VMEM((TAPS * TAPS, COUT, CIN), jnp.float32),
             pltpu.SemaphoreType.DMA((TAPS + 1,)),
             pltpu.SemaphoreType.DMA((TAPS * TAPS,)),
-            pltpu.SemaphoreType.DMA((2,)),
         ],
         compiler_params=pltpu.CompilerParams(vmem_limit_bytes=58 * 1024 * 1024),
-    )(summed, grad, owned)
+    )(summed)
     weight_grad = weight_grad.reshape(TAPS, TAPS, COUT, CIN)
     bias_grad = bias_grad.reshape(COUT)
     out_grad = jnp.transpose(grad, (2, 1, 0))[None]

time: 81.2 us -> 78.7 us (0.969)
  Pallas kernels: 80.4 us -> 75.1 us
  local copies, waits for them, and re-layouts: 0 us -> 2.8 us
    pallas_call x1, Pallas kernels: 7.55 us -> 4.49 us  [body(): pl.pallas_call(finish_kernel, out_shape=[jax.ShapeDtypeStruct((TAPS * TAP...]
    unnamed x0 -> x2, local copies, waits for them, and re-layouts: none -> 2.8 us
    pallas_call x1, Pallas kernels: 72.8 us -> 70.6 us  [body(): pl.pallas_call(whole_kernel, out_shape=[jax.ShapeDtypeStruct((TAPS, ROWS,...]
where the time goes in v8:
time: 78.7 us; the launch traced here: 78.5 us
  Pallas kernels  75.1 us (95%)
  local copies, waits for them, and re-layouts  2.8 us (4%)
    pallas_call x1, Pallas kernels, body(): pl.pallas_call(whole_kernel, out_shape=[jax.ShapeDtypeStruct((TAPS, ROWS,...  70.6 us
    pallas_call x1, Pallas kernels, body(): pl.pallas_call(finish_kernel, out_shape=[jax.ShapeDtypeStruct((TAPS * TAP...  4.49 us
    unnamed x2, local copies, waits for them, and re-layouts  2.8 us

profile of v8, /device:TPU:1, one launch (start us, length us, event | category | flops | bytes accessed | tf_op | source)
XLA Modules:
  0.0 78.5 jit_solution(15065647320763930080)
XLA Ops:
  0.6 70.6 %shard_map.111 = (bf16[5,2048,128]{2,1,0:T(8,128)(2,1)}, bf16[45,16,73]{2,1,0:T(8,128)(2,1)}, f32[1,270]{1,0:T(1,128)}) custom-call(bf16[20,45,641]{2,1,0:T(8,128)(2,1)} %bitcast.16, bf16[5,5,73,641]{3,2,1,0:T(8,128)(2,1)} %w_hbm.1, f32[45,16,73]{2,1,0:T(8,128)} %bitcast.17, bf16[5,64,768]{2,1,0:T(8,128)(2,1)} %constant.4.clone.places_hbm, ...), custom_call_target="tpu_custom_call" | custom-call | flops 6442450944 | bytes 16777216 | tf_op jit(solution)/shard_map/pallas_call | solution.py:662
  71.2 4.5 %shard_map.112 = (f32[25,73,641]{2,1,0:T(8,128)}, f32[1,73]{1,0:T(1,128)}) custom-call(bf16[5,2048,128]{2,1,0:T(8,128)(2,1)} %get-tuple-element.11.summed), custom_call_target="tpu_custom_call" | custom-call | tf_op jit(solution)/shard_map/pallas_call | solution.py:681
  75.7 1.6 %copy.14 = bf16[1,73,16,45]{1,2,3,0:T(8,128)(2,1)} copy(bf16[1,73,16,45]{1,2,3,0:T(8,128)(2,1)} %bitcast.13) | data formatting | bytes 210240
  77.3 1.2 %copy.15 = f32[1,1,270]{2,1,0:T(1,128)} copy(f32[1,1,270]{2,1,0:T(1,128)} %bitcast.14) | data formatting | bytes 2160

commit v9 on v8

--- a/solution.py
+++ b/solution.py
@@ -624,7 +624,8 @@
 
 
 def finish_kernel(
-    summed, weight_grad, bias_grad, main, wide, in_sems, out_sems
+    summed, grad_in, owned_in, weight_grad, grad_out, owned_out, bias_grad,
+    main, wide, grad_here, owned_here, in_sems, out_sems, pass_sems,
 ):
     factor = 1.0 / math.sqrt(MEMBERS * LAT * LON_DEV * GROUPS)
     first = TAPS * TAP_ROWS
@@ -633,7 +634,11 @@
     for a in range(TAPS):
         rows = (slice(None), slice(a * TAP_ROWS, (a + 1) * TAP_ROWS))
         loads.append(pltpu.make_async_copy(summed.at[rows], main.at[rows], in_sems.at[a]))
-    for copy in loads:
+    taken = [
+        pltpu.make_async_copy(grad_in, grad_here, pass_sems.at[0]),
+        pltpu.make_async_copy(owned_in, owned_here, pass_sems.at[1]),
+    ]
+    for copy in loads + taken:
         copy.start()
     loads[0].wait()
     more = main[TAPS - 1, first:ROWS, :].astype(jnp.float32) * factor
@@ -652,7 +657,14 @@
             wide[n, :, WIDE:CIN] = last[b * CHAN : b * CHAN + COUT, 0:1]
             stores.append(pltpu.make_async_copy(wide.at[n], weight_grad.at[n], out_sems.at[n]))
             stores[-1].start()
-    for copy in stores:
+    given = [
+        pltpu.make_async_copy(grad_here, grad_out, pass_sems.at[2]),
+        pltpu.make_async_copy(owned_here, owned_out, pass_sems.at[3]),
+    ]
+    for source, target in zip(taken, given):
+        source.wait()
+        target.start()
+    for copy in stores + given:
         copy.wait()
 
 
@@ -678,22 +690,27 @@
         jnp.asarray(margin_places(), jnp.bfloat16), jnp.asarray(edge_picks(), jnp.bfloat16),
         out_bias.reshape(1, COUT), widths.reshape(1, COUT), owner_start[0],
     )
-    weight_grad, bias_grad = pl.pallas_call(
+    weight_grad, grad, owned, bias_grad = pl.pallas_call(
         finish_kernel,
         out_shape=[
             jax.ShapeDtypeStruct((TAPS * TAPS, COUT, CIN), jnp.float32),
+            jax.ShapeDtypeStruct((LON_DEV, LAT, COUT), jnp.bfloat16),
+            jax.ShapeDtypeStruct((1, CAP * LON_DEV), jnp.float32),
             jax.ShapeDtypeStruct((1, COUT), jnp.float32),
         ],
-        in_specs=[hbm],
-        out_specs=[hbm, vmem],
+        in_specs=[hbm] * 3,
+        out_specs=[hbm] * 3 + [vmem],
         scratch_shapes=[
             pltpu.VMEM((TAPS, ROWS, LANES), jnp.bfloat16),
             pltpu.VMEM((TAPS * TAPS, COUT, CIN), jnp.float32),
+            pltpu.VMEM((LON_DEV, LAT, COUT), jnp.bfloat16),
+            pltpu.VMEM((1, CAP * LON_DEV), jnp.float32),
             pltpu.SemaphoreType.DMA((TAPS + 1,)),
             pltpu.SemaphoreType.DMA((TAPS * TAPS,)),
+            pltpu.SemaphoreType.DMA((4,)),
         ],
         compiler_params=pltpu.CompilerParams(vmem_limit_bytes=58 * 1024 * 1024),
-    )(summed)
+    )(summed, grad, owned)
     weight_grad = weight_grad.reshape(TAPS, TAPS, COUT, CIN)
     bias_grad = bias_grad.reshape(COUT)
     out_grad = jnp.transpose(grad, (2, 1, 0))[None]

time: 78.7 us -> 76 us (0.966)
  local copies, waits for them, and re-layouts: 2.8 us -> 0 us
    unnamed x2 -> x0, local copies, waits for them, and re-layouts: 2.8 us -> none
where the time goes in v9:
time: 76 us; the launch traced here: 75.8 us
  Pallas kernels  75.1 us (99%)
    pallas_call x1, Pallas kernels, body(): pl.pallas_call(whole_kernel, out_shape=[jax.ShapeDtypeStruct((TAPS, ROWS,...  70.6 us
    pallas_call x1, Pallas kernels, body(): pl.pallas_call(finish_kernel, out_shape=[jax.ShapeDtypeStruct((TAPS * TAP...  4.59 us

profile of v9, /device:TPU:1, one launch (start us, length us, event | category | flops | bytes accessed | tf_op | source)
XLA Modules:
  0.0 75.8 jit_solution(13869347331442919201)
XLA Ops:
  0.6 70.6 %shard_map.111 = (bf16[5,2048,128]{2,1,0:T(8,128)(2,1)}, bf16[45,16,73]{2,1,0:T(8,128)(2,1)}, f32[1,270]{1,0:T(1,128)}) custom-call(bf16[20,45,641]{2,1,0:T(8,128)(2,1)} %bitcast.14, bf16[5,5,73,641]{3,2,1,0:T(8,128)(2,1)} %w_hbm.1, f32[45,16,73]{2,1,0:T(8,128)} %bitcast.15, bf16[5,64,768]{2,1,0:T(8,128)(2,1)} %constant.4.clone.places_hbm, ...), custom_call_target="tpu_custom_call" | custom-call | flops 6442450944 | bytes 16777216 | tf_op jit(solution)/shard_map/pallas_call | solution.py:674
  71.2 4.6 %shard_map.112 = (f32[25,73,641]{2,1,0:T(8,128)}, bf16[45,16,73]{2,1,0:T(8,128)(2,1)}, f32[1,270]{1,0:T(1,128)}, f32[1,73]{1,0:T(1,128)}) custom-call(bf16[5,2048,128]{2,1,0:T(8,128)(2,1)} %get-tuple-element.11.summed, bf16[45,16,73]{2,1,0:T(8,128)(2,1)} %get-tuple-element.12.grad_in, f32[1,270]{1,0:T(1,128)} %get-tuple-element.13.owned_in), custom_call_target="tpu_custom_call" | custom-call | tf_op jit(solution)/shard_map/pallas_call | solution.py:693

commit v10 on v9

--- a/solution.py
+++ b/solution.py
@@ -126,6 +126,35 @@
         send(source, rxs[k][s].at[delta - 1], send_sems.at[k, s + 1], recv_sems.at[k, s + 1], there)
 
 
+def launch_pieces(at, k, cur, rxs, send_sems, piece_recv):
+    first, second = ORDERS[k][0], ORDERS[k][1]
+    rows, piece = SIZES[k][0], SIZES[k][1]
+    for dy in (2, 1, 3, 0):
+        for dx in (2, 1, 3):
+            there = moved(at, first, dx)
+            row = there[first] * rows + moved(at, second, dy)[second] * piece
+            source = cur[k][0].at[pl.ds(pl.multiple_of(row, 16), piece)]
+            into = rxs[k][0].at[dx - 1, dy * piece : (dy + 1) * piece]
+            send(source, into, send_sems.at[k, 1], piece_recv.at[k, 4 * dx + dy], there)
+
+
+def pass_piece(at, k, dy, cur, rxs, send_sems, recv_sems, piece_recv):
+    first, second = ORDERS[k][0], ORDERS[k][1]
+    rows, piece = SIZES[k][0], SIZES[k][1]
+    there = moved(at, second, dy)
+    total = cur[k][0][
+        pl.ds(pl.multiple_of(at[first] * rows + there[second] * piece, 16), piece), :
+    ].astype(jnp.float32)
+    for dx in (1, 3, 2):
+        landed = rxs[k][0].at[dx - 1, dy * piece : (dy + 1) * piece]
+        finish(landed, send_sems.at[k, 1], piece_recv.at[k, 4 * dx + dy], at).wait_recv()
+        total = total + landed[...].astype(jnp.float32)
+    here = pl.ds(pl.multiple_of(there[second] * piece, 16), piece)
+    cur[k][1][here, :] = total.astype(jnp.bfloat16)
+    if dy:
+        send(cur[k][1].at[here], rxs[k][1].at[dy - 1], send_sems.at[k, 2], recv_sems.at[k, 2], there)
+
+
 def add_core(at, k, mine, core_rx, cur, send_sems, recv_sems):
     finish(core_rx[k], send_sems.at[k, 0], recv_sems.at[k, 0], at).wait_recv()
     step = 256
@@ -159,7 +188,7 @@
         send(block, block, send_sem, recv_sem, there)
 
 
-def all_reduce(at, out, core_rx, cur, rxs, shared, send_sems, recv_sems, mid_recv, far_recv):
+def all_reduce(at, out, core_rx, cur, rxs, shared, send_sems, recv_sems, mid_recv, far_recv, piece_recv):
     row = [0] * PARTS
     partner = moved(at, "core", 1)
     for s in range(3):
@@ -171,6 +200,13 @@
                     total = total + shared[y].astype(jnp.float32)
                 place(at, out, k, row[k], 32)[...] = total.astype(jnp.bfloat16)
                 gather(at, out, k, 1, row[k], send_sems, recv_sems)
+                continue
+            if s == 0 and k < 2:
+                row[k] = row[k] + at[ORDERS[k][0]] * SIZES[k][0]
+                if k == 1:
+                    for dy in (2, 1, 3, 0):
+                        for part in range(2):
+                            pass_piece(at, part, dy, cur, rxs, send_sems, recv_sems, piece_recv)
                 continue
             axis, rows = ORDERS[k][s], SIZES[k][s]
             finish(rxs[k][s], send_sems.at[k, s + 1], recv_sems.at[k, s + 1], at).wait_recv()
@@ -259,6 +295,7 @@
     shapes.append(pltpu.VMEM((4, 32, LANES), jnp.bfloat16))
     shapes += [pltpu.SemaphoreType.DMA((PARTS, 8)), pltpu.SemaphoreType.DMA((PARTS, 8))]
     shapes += [pltpu.SemaphoreType.DMA((2, 4)), pltpu.SemaphoreType.DMA((2, 16))]
+    shapes.append(pltpu.SemaphoreType.DMA((2, 16)))
     return shapes
 
 
@@ -511,7 +548,7 @@
     core_rx, rest = scratch[21:24], scratch[24:]
     cur = [rest[3 * k : 3 * k + 3] for k in range(PARTS)]
     rxs = [rest[8 + 3 * k : 11 + 3 * k] for k in range(PARTS)]
-    shared, send_sems, recv_sems, mid_recv, far_recv = rest[16:21]
+    shared, send_sems, recv_sems, mid_recv, far_recv, piece_recv = rest[16:22]
     at = position()
     member, lon = lax.axis_index("member"), lax.axis_index("lon")
     ahead = (member, lax.rem(lon + 1, GROUPS))
@@ -574,11 +611,14 @@
     weight_terms(core, x, margin, stacked, edge_stacked, mine)
     for k, own in ((0, mine), (1, mine), (2, fifth)):
         add_core(at, k, own, core_rx, cur, send_sems, recv_sems)
-        launch(at, k, 0, cur, rxs, send_sems, recv_sems)
+        if k == 2:
+            launch(at, k, 0, cur, rxs, send_sems, recv_sems)
+        else:
+            launch_pieces(at, k, cur, rxs, send_sems, piece_recv)
     write_gradient(packed, grad_out)
     finish(score_rx.at[0:7], near_send.at[4], near_recv.at[4], at).wait_recv()
     own_scores(starts, score_rx, owned)
-    all_reduce(at, out, core_rx, cur, rxs, shared, send_sems, recv_sems, mid_recv, far_recv)
+    all_reduce(at, out, core_rx, cur, rxs, shared, send_sems, recv_sems, mid_recv, far_recv, piece_recv)
     finish(values.at[0:7], near_send.at[2], near_recv.at[2], at).wait_send()
     finish(gathered.at[0:7], near_send.at[3], near_recv.at[3], at).wait_send()
     finish(score_rx.at[0:7], near_send.at[4], near_recv.at[4], at).wait_send()

time: 76 us -> 76 us (level)
  no operation moved by 1% of the time
where the time goes in v10:
time: 76 us; the launch traced here: 75.8 us
  Pallas kernels  75.2 us (99%)
    pallas_call x1, Pallas kernels, body(): pl.pallas_call(whole_kernel, out_shape=[jax.ShapeDtypeStruct((TAPS, ROWS,...  70.6 us
    pallas_call x1, Pallas kernels, body(): pl.pallas_call(finish_kernel, out_shape=[jax.ShapeDtypeStruct((TAPS * TAP...  4.59 us

profile of v10, /device:TPU:1, one launch (start us, length us, event | category | flops | bytes accessed | tf_op | source)
XLA Modules:
  0.0 75.8 jit_solution(4678798926702888943)
XLA Ops:
  0.6 70.6 %shard_map.111 = (bf16[5,2048,128]{2,1,0:T(8,128)(2,1)}, bf16[45,16,73]{2,1,0:T(8,128)(2,1)}, f32[1,270]{1,0:T(1,128)}) custom-call(bf16[20,45,641]{2,1,0:T(8,128)(2,1)} %bitcast.14, bf16[5,5,73,641]{3,2,1,0:T(8,128)(2,1)} %w_hbm.1, f32[45,16,73]{2,1,0:T(8,128)} %bitcast.15, bf16[5,64,768]{2,1,0:T(8,128)(2,1)} %constant.4.clone.places_hbm, ...), custom_call_target="tpu_custom_call" | custom-call | flops 6442450944 | bytes 16777216 | tf_op jit(solution)/shard_map/pallas_call | solution.py:714
  71.3 4.6 %shard_map.112 = (f32[25,73,641]{2,1,0:T(8,128)}, bf16[45,16,73]{2,1,0:T(8,128)(2,1)}, f32[1,270]{1,0:T(1,128)}, f32[1,73]{1,0:T(1,128)}) custom-call(bf16[5,2048,128]{2,1,0:T(8,128)(2,1)} %get-tuple-element.11.summed, bf16[45,16,73]{2,1,0:T(8,128)(2,1)} %get-tuple-element.12.grad_in, f32[1,270]{1,0:T(1,128)} %get-tuple-element.13.owned_in), custom_call_target="tpu_custom_call" | custom-call | tf_op jit(solution)/shard_map/pallas_call | solution.py:733

commit v11 on v9

--- a/solution.py
+++ b/solution.py
@@ -374,17 +374,21 @@
     edge_taps[...] = lax.fori_loop(0, TAPS, one, jnp.zeros((TAP_ROWS, 64), jnp.float32))
 
 
-def convolved(taps, edge_taps, places, bias):
+def sum_own(taps, bias):
     total = jnp.broadcast_to(bias, (CHAN, POINTS))
     for b in range(TAPS):
-        rows = slice(b * CHAN, b * CHAN + CHAN)
-        part = taps[rows, :]
+        part = taps[b * CHAN : (b + 1) * CHAN, :]
         total = total + (part if b == 2 else pltpu.roll(part, (2 - b) % POINTS, 1))
-        if b != 2:
-            total = total + jnp.dot(
-                edge_taps[rows, :], places[b].astype(jnp.float32),
-                precision=lax.Precision.HIGHEST, preferred_element_type=jnp.float32,
-            )
+    taps[0:CHAN, :] = total
+
+
+def convolved(taps, edge_taps, places):
+    total = taps[0:CHAN, :]
+    for b in (0, 1, 3, 4):
+        total = total + jnp.dot(
+            edge_taps[b * CHAN : (b + 1) * CHAN, :], places[b].astype(jnp.float32),
+            precision=lax.Precision.HIGHEST, preferred_element_type=jnp.float32,
+        )
     return total
 
 
@@ -540,6 +544,7 @@
     send_to(edges.at[0], halo.at[0], near_send.at[0], near_recv.at[0], ahead)
     send_to(edges.at[1], halo.at[1], near_send.at[1], near_recv.at[1], behind)
     forward_own(x, staged, taps)
+    sum_own(taps, vectors[...][:, 0:1])
     loads[3].wait()
     loads[4].wait()
     stage_target(observed, wide, target)
@@ -547,7 +552,7 @@
     finish(halo.at[1], near_send.at[1], near_recv.at[1], at).wait()
     stage_margin(halo, margin)
     forward_margin(margin, staged, edge_taps)
-    outputs = convolved(taps, edge_taps, places, vectors[...][:, 0:1])
+    outputs = convolved(taps, edge_taps, places)
     for q in range(MEMBERS):
         to_score[q, :, 0:CHUNK] = outputs[:, q * CHUNK : (q + 1) * CHUNK].astype(jnp.bfloat16)
         to_score[q, :, CHUNK:LANES] = jnp.zeros((CHAN, LANES - CHUNK), jnp.bfloat16)

time: 76 us -> 76.3 us (level)
  no operation moved by 1% of the time
where the time goes in v11:
time: 76.3 us; the launch traced here: 76.1 us
  Pallas kernels  75.5 us (99%)
    pallas_call x1, Pallas kernels, body(): pl.pallas_call(whole_kernel, out_shape=[jax.ShapeDtypeStruct((TAPS, ROWS,...  70.9 us
    pallas_call x1, Pallas kernels, body(): pl.pallas_call(finish_kernel, out_shape=[jax.ShapeDtypeStruct((TAPS * TAP...  4.59 us

profile of v11, /device:TPU:1, one launch (start us, length us, event | category | flops | bytes accessed | tf_op | source)
XLA Modules:
  0.0 76.1 jit_solution(964347591420259207)
XLA Ops:
  0.6 70.9 %shard_map.111 = (bf16[5,2048,128]{2,1,0:T(8,128)(2,1)}, bf16[45,16,73]{2,1,0:T(8,128)(2,1)}, f32[1,270]{1,0:T(1,128)}) custom-call(bf16[20,45,641]{2,1,0:T(8,128)(2,1)} %bitcast.14, bf16[5,5,73,641]{3,2,1,0:T(8,128)(2,1)} %w_hbm.1, f32[45,16,73]{2,1,0:T(8,128)} %bitcast.15, bf16[5,64,768]{2,1,0:T(8,128)(2,1)} %constant.4.clone.places_hbm, ...), custom_call_target="tpu_custom_call" | custom-call | flops 6442450944 | bytes 16777216 | tf_op jit(solution)/shard_map/pallas_call | solution.py:679
  71.5 4.6 %shard_map.112 = (f32[25,73,641]{2,1,0:T(8,128)}, bf16[45,16,73]{2,1,0:T(8,128)(2,1)}, f32[1,270]{1,0:T(1,128)}, f32[1,73]{1,0:T(1,128)}) custom-call(bf16[5,2048,128]{2,1,0:T(8,128)(2,1)} %get-tuple-element.11.summed, bf16[45,16,73]{2,1,0:T(8,128)(2,1)} %get-tuple-element.12.grad_in, f32[1,270]{1,0:T(1,128)} %get-tuple-element.13.owned_in), custom_call_target="tpu_custom_call" | custom-call | tf_op jit(solution)/shard_map/pallas_call | solution.py:698
